TPU v7x, 32 devices: a whole 2x2x4 slice. The times are simulated.
32 devices in a mesh: groups: 2 (over y), ctx: 4 (over z), exp: 4 (over x, core).
Axes of the slice: x: 2, y: 2, z: 4, core: 2. Of those that a mesh axis runs over, the one named last changes fastest.
Arguments:
- tokens: bfloat16 [1024, 2048], P(('groups', 'ctx')), parts along dimension 0, may hold values from -6 to 6
- positions: int32 [1024], P(('groups', 'ctx')), parts along dimension 0, may hold values from 0 to 511, as said below
- attn_gain: float32 [2048], replicated, may hold values from 0.1 to 1.9
- w_qkv: bfloat16 [2048, 16, 384], P(None, 'exp')
- w_out: bfloat16 [16, 128, 2048], P('exp'), may hold values from -0.5 to 0.5
- moe_gain: float32 [2048], replicated, may hold values from 0.1 to 1.9
- expert_ids: int32 [1024, 6], P(('groups', 'ctx', 'exp')), parts along dimension 0, may hold values from 0 to 63, as said below
- gate_probs: float32 [1024, 6], P(('groups', 'ctx', 'exp')), parts along dimension 0, may hold values from 0.1 to 1
- w_gate: bfloat16 [4, 2048, 768], P('exp', 'ctx'), may hold values from -0.125 to 0.125
- w_up: bfloat16 [4, 2048, 768], P('exp', 'ctx'), may hold values from -0.125 to 0.125
- w_down: bfloat16 [4, 768, 2048], P('exp', None, 'ctx'), may hold values from -0.21875 to 0.21875
Outputs:
- mixed: bfloat16 [1024, 2048], P(('groups', 'ctx', 'exp')), parts along dimension 0
There are 2 independent parts, one for each index of `groups`. A program takes and returns all parts, laid end to end along the dimension named above; an argument that names none is the same for every part. Nothing has to cross between parts.
Inputs may be any that keep to these rules, and one draw needn't show every extreme that they name: `positions`: each of 0 to 511 once: a prefix in order, then a suffix in order, then the middle in order. `expert_ids`: each row names 6 different experts; in each aligned block of 32 rows (the rows of one device) no expert is named by more than 6 rows, and one expert below 4 is named by exactly 6 rows in every block.
All inputs are finite; a program needn't handle non-finite values.
Results may differ from a plain program's by a relative error of at most 0.011.
Values may be sent and summed in bfloat16 or wider, within the bound.
A program may use at most 128 MiB of HBM per device.

v0:
```python
import jax
import jax.numpy as jnp
from jax import lax
from jax.sharding import PartitionSpec as P

CAP = 6


epsilon = 1e-06


def rms_norm(rows, gain):
    rows = rows.astype(jnp.float32)
    return rows * lax.rsqrt(jnp.mean(rows * rows, axis=-1, keepdims=True) + epsilon) * gain


def rotary_tables(positions, width):
    freqs = 10000.0 ** (-jnp.arange(width // 2, dtype=jnp.float32) * 2.0 / width)
    angles = positions.astype(jnp.float32)[:, None] * freqs[None, :]
    return (jnp.cos(angles), jnp.sin(angles))


def rotate(vectors, cosines, sines):
    half = vectors.shape[-1] // 2
    first = vectors[..., :half]
    second = vectors[..., half:]
    return jnp.concatenate(
        [first * cosines - second * sines, second * cosines + first * sines], axis=-1
    )


def update(carry, pieces, rows, row_order, scale):
    peak, total, summed = carry
    key_piece, value_piece = pieces
    scores = jnp.einsum("hqc,hkc->hqk", rows, key_piece, preferred_element_type=jnp.float32) * scale
    key_order = jnp.arange(key_piece.shape[1], dtype=jnp.int32)
    allowed = key_order[None, :] <= row_order[:, None]
    scores = jnp.where(allowed[None], scores, -jnp.inf)
    new_peak = jnp.max(scores, axis=2)
    safe_peak = jnp.where(jnp.isfinite(new_peak), new_peak, 0.0)
    probs = jnp.exp(scores - safe_peak[..., None])
    factor = jnp.exp(peak - safe_peak)
    weights = probs.astype(jnp.bfloat16)
    summed = summed * factor[..., None] + jnp.einsum(
        "hqk,hkc->hqc", weights, value_piece, preferred_element_type=jnp.float32
    )
    total = total * factor + jnp.sum(probs, axis=2)
    return (new_peak, total, summed)


def empty_state(heads_here, rows_count, head_dim):
    return (
        jnp.full((heads_here, rows_count), -jnp.inf, jnp.float32),
        jnp.zeros((heads_here, rows_count), jnp.float32),
        jnp.zeros((heads_here, rows_count, head_dim), jnp.float32),
    )


def body(
    tokens,
    positions,
    attn_gain,
    w_qkv,
    w_out,
    moe_gain,
    expert_ids,
    gate_probs,
    w_gate,
    w_up,
    w_down,
):
    seq_dev = tokens.shape[0]
    width = tokens.shape[1]
    head_dim = w_out.shape[1]
    heads_here = w_out.shape[0]
    normed = rms_norm(tokens, attn_gain).astype(jnp.bfloat16)
    projected = jnp.einsum("sd,dhc->hsc", normed, w_qkv, preferred_element_type=jnp.float32)
    cosines, sines = rotary_tables(positions, head_dim)
    queries = rotate(projected[..., :head_dim], cosines, sines).astype(jnp.bfloat16)
    key_rows = rotate(projected[..., head_dim : 2 * head_dim], cosines, sines).astype(jnp.bfloat16)
    value_rows = projected[..., 2 * head_dim :].astype(jnp.bfloat16)
    first_query = lax.axis_index("ctx") * seq_dev
    query_order = first_query + jnp.arange(seq_dev, dtype=jnp.int32)
    scale = head_dim ** (-0.5)
    init = empty_state(heads_here, seq_dev, head_dim)
    folded = update(
        init,
        (
            lax.all_gather(key_rows, "ctx", axis=1, tiled=True),
            lax.all_gather(value_rows, "ctx", axis=1, tiled=True),
        ),
        queries,
        query_order,
        scale,
    )
    attended = (folded[2] / folded[1][..., None]).astype(jnp.bfloat16)
    exp_rows = seq_dev // lax.axis_size("exp")
    attn_rows = lax.psum_scatter(
        jnp.einsum("hsc,hcd->sd", attended, w_out, preferred_element_type=jnp.float32).astype(
            jnp.bfloat16
        ),
        "exp",
        scatter_dimension=0,
        tiled=True,
    ).astype(jnp.float32)
    own_tokens = lax.dynamic_slice_in_dim(
        tokens, lax.axis_index("exp") * exp_rows, exp_rows, 0
    ).astype(jnp.float32)
    residual = own_tokens + attn_rows
    normed_moe = rms_norm(residual, moe_gain).astype(jnp.bfloat16)
    flight = lax.axis_size("exp")
    slot_count = flight * CAP
    flat_ids = expert_ids.reshape(-1)
    in_flight = flat_ids < flight
    expert_marks = (
        (flat_ids[:, None] == jnp.arange(flight, dtype=jnp.int32)[None, :]) & in_flight[:, None]
    ).astype(jnp.int32)
    earlier = jnp.cumsum(expert_marks, axis=0) - expert_marks
    place_in = jnp.sum(earlier * expert_marks, axis=1)
    slot_of = jnp.where(in_flight, flat_ids * CAP + place_in, -1).reshape(expert_ids.shape)
    slot_hits = slot_of[:, :, None] == jnp.arange(slot_count, dtype=jnp.int32)[None, None, :]
    send_matrix = jnp.sum(slot_hits.astype(jnp.int32), axis=1).astype(jnp.bfloat16)
    combine_matrix = jnp.sum(jnp.where(slot_hits, gate_probs[:, :, None], 0.0), axis=1)
    outgoing = jnp.einsum(
        "ts,td->sd", send_matrix, normed_moe, preferred_element_type=jnp.float32
    ).astype(jnp.bfloat16)
    incoming = lax.all_to_all(
        outgoing.reshape(flight, CAP, width), "exp", split_axis=0, concat_axis=0, tiled=True
    )
    routed_rows = incoming.reshape(-1, width)
    gate_next = jnp.dot(
        routed_rows,
        lax.all_gather(w_gate, "ctx", axis=1, tiled=True)[0],
        preferred_element_type=jnp.float32,
    )
    up_next = jnp.dot(
        routed_rows,
        lax.all_gather(w_up, "ctx", axis=1, tiled=True)[0],
        preferred_element_type=jnp.float32,
    )
    hidden = (jax.nn.silu(gate_next) * up_next).astype(jnp.bfloat16)
    expert_out = jnp.dot(
        hidden,
        lax.all_gather(w_down, "ctx", axis=2, tiled=True)[0],
        preferred_element_type=jnp.float32,
    ).astype(jnp.bfloat16)
    returned = lax.all_to_all(
        expert_out.reshape(flight, CAP, width), "exp", split_axis=0, concat_axis=0, tiled=True
    )
    moe_sum = jnp.dot(
        combine_matrix,
        returned.reshape(slot_count, width).astype(jnp.float32),
        precision=lax.Precision.HIGHEST,
    )
    return (residual + moe_sum).astype(jnp.bfloat16)


def solution(mesh):
    return jax.shard_map(
        body,
        mesh=mesh,
        in_specs=(
            P(("groups", "ctx"), None),
            P(("groups", "ctx")),
            P(),
            P(None, "exp", None),
            P("exp", None, None),
            P(),
            P(("groups", "ctx", "exp"), None),
            P(("groups", "ctx", "exp"), None),
            P("exp", "ctx", None),
            P("exp", "ctx", None),
            P("exp", None, "ctx"),
        ),
        out_specs=P(("groups", "ctx", "exp"), None),
        check_vma=False,
    )
```

profile of v0, /device:TPU:0, one launch (start us, length us, event | category | flops | bytes accessed | tf_op | source)
XLA Modules:
  0.0 268.0 jit_solution(12947201612573671402)
XLA Ops:
  7.4 1.4 fusion.25
  8.8 0.7 convert_element_type.56
  9.4 4.0 %fusion.14 = f32[4,128,384]{2,1,0:T(8,128)S(1)} fusion(bf16[2048,4,384]{2,1,0:T(4,128)(2,1)} %param.14, bf16[128,2048]{1,0:T(8,128)(2,1)} %param.11, f32[2048]{0:T(1024)} %param.13, f32[128]{0:T(128)S(1)} %add_rsqrt_fusion.1), kind=kOutput, calls=%fused_computation.18 | convolution fusion | flops 806354944 | bytes 7610880 | tf_op jit(solution)/shard_map/sd,dhc->hsc/dot_general | solution.py:77
  13.5 0.3 multiply_cosine_fusion
  13.8 0.3 subtract_convert_fusion.1
  14.1 0.1 pad_maximum_fusion
  14.2 18.0 %all_gather.15 = bf16[4,512,128]{2,1,0:T(8,128)(2,1)} all-gather(bf16[4,128,128]{2,1,0:T(8,128)(2,1)S(1)} %pad_maximum_fusion), channel_id=1, replica_groups=mesh['groups'=2,'ctx'=4,'exp'=4] {'ctx'}, dimensions={1}, use_global_device_ids=true | all-gather | bytes 655360 | tf_op jit(solution)/shard_map/all_gather | solution.py:89
  32.2 0.1 iota_compare_fusion
  32.3 1.5 fusion.63
  33.8 0.3 fusion.30
  34.2 17.0 %all_gather.16 = bf16[4,512,128]{2,1,0:T(8,128)(2,1)} all-gather(bf16[4,128,128]{2,1,0:T(8,128)(2,1)S(1)} %slice.60), channel_id=1, replica_groups=mesh['groups'=2,'ctx'=4,'exp'=4] {'ctx'}, dimensions={1}, use_global_device_ids=true | all-gather | bytes 655360 | tf_op jit(solution)/shard_map/all_gather | solution.py:90
  51.2 2.6 fusion.8
  53.9 0.5 all-gather.4.cloned.1.call-update
  54.4 0.5 all-gather.6.cloned.1.call-update
  55.0 0.5 all-gather.8.cloned.1.call-update
  55.7 0.1 eq.35
  55.8 1.2 reduce-window.6
  57.1 0.1 copy.28
  57.5 0.1 reduce_sum.59
  57.7 18.5 %reduce-scatter.2.cloned.1.call-done = bf16[32,2048]{1,0:T(8,128)(2,1)} async-done(((bf16[128,2048]{1,0:T(8,128)(2,1)}), bf16[32,2048]{1,0:T(8,128)(2,1)}) %reduce-scatter.2.cloned.1.call-update) | async-done | bytes 131088 | tf_op jit(solution)/shard_map/reduce_scatter | solution.py:98
  76.2 1.1 multiply_reduce_fusion
  77.3 1.1 convolution_convert_fusion
  78.5 7.0 %all_to_all.10 = bf16[4,6,2048]{2,1,0:T(8,128)(2,1)S(1)} all-to-all(bf16[4,6,2048]{2,1,0:T(8,128)(2,1)S(1)} %reshape.153), channel_id=1, replica_groups=mesh['groups'=2,'ctx'=4,'exp'=4] {'exp'}, dimensions={0} | all-to-all | bytes 196608 | tf_op jit(solution)/shard_map/all_to_all | solution.py:127
  85.6 34.3 %all-gather.4.cloned.1.call-done = bf16[1,2048,768]{2,1,0:T(8,128)(2,1)} async-done(((bf16[1,512,768]{2,1,0:T(8,128)(2,1)}), bf16[1,2048,768]{2,1,0:T(8,128)(2,1)}) %all-gather.4.cloned.1.call-update) | async-done | bytes 3145744 | tf_op jit(solution)/shard_map/all_gather | solution.py:133
  119.9 2.4 fusion.6
  122.3 61.0 %all-gather.6.cloned.1.call-done = bf16[1,2048,768]{2,1,0:T(8,128)(2,1)} async-done(((bf16[1,512,768]{2,1,0:T(8,128)(2,1)}), bf16[1,2048,768]{2,1,0:T(8,128)(2,1)}) %all-gather.6.cloned.1.call-update) | async-done | bytes 3145744 | tf_op jit(solution)/shard_map/all_gather | solution.py:138
  183.4 63.4 %all-gather.8.cloned.1.call-done = bf16[1,768,2048]{2,1,0:T(8,128)(2,1)} async-done(((bf16[1,768,512]{2,1,0:T(8,128)(2,1)}), bf16[1,768,2048]{2,1,0:T(8,128)(2,1)}) %all-gather.8.cloned.1.call-update) | async-done | bytes 3145744 | tf_op jit(solution)/shard_map/all_gather | solution.py:144
  246.8 4.0 %fusion.10 = bf16[24,2048]{1,0:T(8,128)(2,1)S(1)} fusion(bf16[1,768,2048]{2,1,0:T(8,128)(2,1)} %all-gather.8.cloned.1.call-done, bf16[24,2048]{1,0:T(8,128)(2,1)S(1)} %reshape.154, bf16[1,2048,768]{2,1,0:T(8,128)(2,1)} %all-gather.6.cloned.1.call-done, f32[24,768]{1,0:T(8,128)S(1)} %fusion.6), kind=kOutput, calls=%fused_computation.12 | convolution fusion | flops 151154688 | bytes 6561792 | tf_op jit(solution)/shard_map/dot_general | solution.py:142
  250.8 0.7 reshape.155
  251.5 3.3 %all-to-all-start.1 = ((bf16[4,6,2048]{2,1,0:T(8,128)(2,1)}), bf16[4,6,2048]{2,1,0:T(8,128)(2,1)S(1)}, u32[]{:S(2)}, u32[]{:S(2)}) async-start(bf16[4,6,2048]{2,1,0:T(8,128)(2,1)} %reshape.155), calls=%async_computation.2 | async-start | bytes 262144 | tf_op jit(solution)/shard_map/all_to_all | solution.py:147
  254.8 4.6 %all-to-all-done.1 = bf16[4,6,2048]{2,1,0:T(8,128)(2,1)S(1)} async-done(((bf16[4,6,2048]{2,1,0:T(8,128)(2,1)}), bf16[4,6,2048]{2,1,0:T(8,128)(2,1)S(1)}, u32[]{:S(2)}, u32[]{:S(2)}) %all-to-all-start.1) | async-done | bytes 98336 | tf_op jit(solution)/shard_map/all_to_all | solution.py:147
  259.5 1.0 fusion.9
  (43 shorter events, 0.9 us)
Async XLA Ops:
  7.4 43.8 %copy-start = (bf16[4,128,2048]{2,1,0:T(8,128)(2,1)S(1)}, bf16[4,128,2048]{2,1,0:T(8,128)(2,1)}, u32[]{:S(2)}) copy-start(bf16[4,128,2048]{2,1,0:T(8,128)(2,1)} %param.15) | copy-start | bytes 6291460
  7.4 68.9 %reduce-scatter.2.cloned.1.call-start = ((), (), s32[]{:S(2)}) async-start(), calls=%async_computation.3 | async-start | bytes 655360 | tf_op jit(solution)/shard_map/reduce_scatter | solution.py:98
  51.2 4.4 %copy-start.4 = (s32[32,6]{0,1:T(8,128)S(1)}, s32[32,6]{0,1:T(8,128)}, u32[]{:S(2)}) copy-start(s32[32,6]{0,1:T(8,128)} %param.17) | copy-start | bytes 2308
  51.2 26.1 %copy-start.3 = (f32[2048]{0:T(1024)S(1)}, f32[2048]{0:T(1024)}, u32[]{:S(2)}) copy-start(f32[2048]{0:T(1024)} %param.16) | copy-start | bytes 24580
  53.8 22.4 %copy-start.1 = (bf16[128,2048]{1,0:T(8,128)(2,1)S(1)}, bf16[128,2048]{1,0:T(8,128)(2,1)}, u32[]{:S(2)}) copy-start(bf16[128,2048]{1,0:T(8,128)(2,1)} %param.11) | copy-start | bytes 1572868
  53.8 66.1 %all-gather.4.cloned.1.call-start = ((), (), s32[]{:S(2)}) async-start(), calls=%async_computation.4 | async-start | bytes 3932160 | tf_op jit(solution)/shard_map/all_gather | solution.py:133
  54.4 129.0 %all-gather.6.cloned.1.call-start = ((), (), s32[]{:S(2)}) async-start(), calls=%async_computation.5 | async-start | bytes 3932160 | tf_op jit(solution)/shard_map/all_gather | solution.py:138
  55.0 191.8 %all-gather.8.cloned.1.call-start = ((), (), s32[]{:S(2)}) async-start(), calls=%async_computation.6 | async-start | bytes 3932160 | tf_op jit(solution)/shard_map/all_gather | solution.py:144
  122.3 132.5 %copy-start.5 = (f32[32,6]{0,1:T(8,128)S(1)}, f32[32,6]{0,1:T(8,128)}, u32[]{:S(2)}) copy-start(f32[32,6]{0,1:T(8,128)} %param.18) | copy-start | bytes 2308
  122.3 137.1 %copy-start.2 = (bf16[32,2048]{1,0:T(8,128)(2,1)S(1)}, bf16[32,2048]{1,0:T(8,128)(2,1)}, u32[]{:S(2)}) copy-start(bf16[32,2048]{1,0:T(8,128)(2,1)} %reduce-scatter.2.cloned.1.call-done) | copy-start | bytes 393220
  251.5 7.9 %all-to-all-start.1 = ((bf16[4,6,2048]{2,1,0:T(8,128)(2,1)}), bf16[4,6,2048]{2,1,0:T(8,128)(2,1)S(1)}, u32[]{:S(2)}, u32[]{:S(2)}) async-start(bf16[4,6,2048]{2,1,0:T(8,128)(2,1)} %reshape.155), calls=%async_computation.2 | async-start | bytes 262144 | tf_op jit(solution)/shard_map/all_to_all | solution.py:147
Sparse Core Ops, SparseCore 0:
  53.9 22.2 reduce-scatter.1
Sparse Core Ops, SparseCore 1:
  55.9 64.0 all-gather.3
  121.3 62.0 all-gather.5
  184.8 61.9 all-gather.7
where the time goes:
time: 268 us
  waiting for transfers between devices  183 us (68%)
  blocking collectives  42 us (16%)
  matrix products  16.6 us (6%)
  between operations  15.2 us (6%)
  other arithmetic  5.68 us (2%)
  starting transfers between devices  3.45 us (1%)
    all_gather x1, waiting for transfers between devices, body(): lax.all_gather(w_down, 'ctx', axis=2, tiled=True)[0]  63.4 us
    all_gather x1, waiting for transfers between devices, body(): lax.all_gather(w_up, 'ctx', axis=1, tiled=True)[0]  61 us
    all_gather x1, waiting for transfers between devices, body(): lax.all_gather(w_gate, 'ctx', axis=1, tiled=True)[0]  34.3 us
    reduce_scatter x1, waiting for transfers between devices, body(): lax.psum_scatter(jnp.einsum('hsc,hcd->sd', attended, w_out, preferred_ele...  18.5 us
    all_gather x1, blocking collectives, body(): lax.all_gather(key_rows, 'ctx', axis=1, tiled=True)  18 us
    all_gather x1, blocking collectives, body(): lax.all_gather(value_rows, 'ctx', axis=1, tiled=True)  17 us
    all_to_all x1, blocking collectives, body(): lax.all_to_all(outgoing.reshape(flight, CAP, width), 'exp', split_axis=0,...  7.02 us
  transfers between devices with their start and end apart: 5, of which 5 were waited for; matrix products, arithmetic and copies ran while one was open for 3% of the time, Pallas kernels for 0%

commit v1 on v0

--- a/solution.py
+++ b/solution.py
@@ -124,29 +124,40 @@
     outgoing = jnp.einsum(
         "ts,td->sd", send_matrix, normed_moe, preferred_element_type=jnp.float32
     ).astype(jnp.bfloat16)
+    n_ctx = lax.axis_size("ctx")
+    columns = width // n_ctx
+    by_device = outgoing.reshape(flight, CAP, n_ctx, columns).transpose(2, 0, 1, 3)
     incoming = lax.all_to_all(
-        outgoing.reshape(flight, CAP, width), "exp", split_axis=0, concat_axis=0, tiled=True
+        by_device.reshape(n_ctx * flight, CAP, columns),
+        ("ctx", "exp"),
+        split_axis=0,
+        concat_axis=0,
+        tiled=True,
     )
-    routed_rows = incoming.reshape(-1, width)
-    gate_next = jnp.dot(
+    routed_rows = incoming.reshape(-1, columns)
+    gate_up = jnp.dot(
         routed_rows,
-        lax.all_gather(w_gate, "ctx", axis=1, tiled=True)[0],
+        jnp.concatenate([w_gate[0], w_up[0]], axis=1),
         preferred_element_type=jnp.float32,
     )
-    up_next = jnp.dot(
-        routed_rows,
-        lax.all_gather(w_up, "ctx", axis=1, tiled=True)[0],
-        preferred_element_type=jnp.float32,
+    gate_up = lax.psum_scatter(gate_up, "ctx", scatter_dimension=0, tiled=True)
+    hidden_width = w_gate.shape[2]
+    hidden = (jax.nn.silu(gate_up[:, :hidden_width]) * gate_up[:, hidden_width:]).astype(
+        jnp.bfloat16
     )
-    hidden = (jax.nn.silu(gate_next) * up_next).astype(jnp.bfloat16)
     expert_out = jnp.dot(
-        hidden,
-        lax.all_gather(w_down, "ctx", axis=2, tiled=True)[0],
+        lax.all_gather(hidden, "ctx", axis=0, tiled=True),
+        w_down[0],
         preferred_element_type=jnp.float32,
     ).astype(jnp.bfloat16)
     returned = lax.all_to_all(
-        expert_out.reshape(flight, CAP, width), "exp", split_axis=0, concat_axis=0, tiled=True
+        expert_out.reshape(n_ctx * flight, CAP, columns),
+        ("ctx", "exp"),
+        split_axis=0,
+        concat_axis=0,
+        tiled=True,
     )
+    returned = returned.reshape(n_ctx, flight, CAP, columns).transpose(1, 2, 0, 3)
     moe_sum = jnp.dot(
         combine_matrix,
         returned.reshape(slot_count, width).astype(jnp.float32),

time: 268 us -> 147 us (0.55)
  waiting for transfers between devices: 183 us -> 47.7 us
  blocking collectives: 42 us -> 60.3 us
  matrix products: 16.6 us -> 13 us
    all_gather x3 -> x0, waiting for transfers between devices: 159 us -> none  [the longest x1 63.4 us: body(): lax.all_gather(w_down, 'ctx', axis=2, tiled=True)[0]]
    reduce_scatter x0 -> x1, waiting for transfers between devices: none -> 19.7 us  [body(): gate_up = lax.psum_scatter(gate_up, 'ctx', scatter_dimension=0, tiled=True)]
    all_gather x0 -> x1, blocking collectives: none -> 13.4 us  [body(): lax.all_gather(hidden, 'ctx', axis=0, tiled=True)]
    all_to_all x1, blocking collectives: 7.02 us -> 12.6 us  [body(): lax.all_to_all(by_device.reshape(n_ctx * flight, CAP, columns), ('ctx', '...]
    dot_general x2, matrix products: 6.39 us -> 2.83 us  [the longest x1 2.57 us: body(): jnp.dot(routed_rows, jnp.concatenate([w_gate[0], w_up[0]], axis=1), prefe...]
    all_to_all x1, waiting for transfers between devices: 4.56 us -> 7.86 us  [body(): lax.all_to_all(expert_out.reshape(n_ctx * flight, CAP, columns), ('ctx',...]
  transfers between devices with their start and end apart: 5 -> 3, of which waited for: 5 -> 3; matrix products, arithmetic and copies ran while one was open for 3% -> 1% of each run, Pallas kernels for 0% -> 0%
where the time goes in v1:
time: 147 us; the launch traced here: 146 us
  blocking collectives  60.3 us (41%)
  waiting for transfers between devices  47.7 us (32%)
  between operations  13.7 us (9%)
  matrix products  13 us (9%)
  other arithmetic  6.68 us (5%)
  starting transfers between devices  3.56 us (2%)
  local copies, waits for them, and re-layouts  1.62 us (1%)
    reduce_scatter x1, waiting for transfers between devices, body(): lax.psum_scatter(jnp.einsum('hsc,hcd->sd', attended, w_out, preferred_ele...  20.1 us
    reduce_scatter x1, waiting for transfers between devices, body(): gate_up = lax.psum_scatter(gate_up, 'ctx', scatter_dimension=0, tiled=True)  19.7 us
    all_gather x1, blocking collectives, body(): lax.all_gather(key_rows, 'ctx', axis=1, tiled=True)  17.4 us
    all_gather x1, blocking collectives, body(): lax.all_gather(value_rows, 'ctx', axis=1, tiled=True)  17 us
    all_gather x1, blocking collectives, body(): lax.all_gather(hidden, 'ctx', axis=0, tiled=True)  13.4 us
    all_to_all x1, blocking collectives, body(): lax.all_to_all(by_device.reshape(n_ctx * flight, CAP, columns), ('ctx', '...  12.6 us
    all_to_all x1, waiting for transfers between devices, body(): lax.all_to_all(expert_out.reshape(n_ctx * flight, CAP, columns), ('ctx',...  7.86 us
    dot_general x1, matrix products, body(): jnp.einsum('sd,dhc->hsc', normed, w_qkv, preferred_element_type=jnp.float32)  4.04 us
  transfers between devices with their start and end apart: 3, of which 3 were waited for; matrix products, arithmetic and copies ran while one was open for 1% of the time, Pallas kernels for 0%

profile of v1, /device:TPU:0, one launch (start us, length us, event | category | flops | bytes accessed | tf_op | source)
XLA Modules:
  0.0 146.5 jit_solution(15902301473270282929)
XLA Ops:
  6.6 0.8 convert_element_type.56
  7.4 1.2 fusion.14
  8.6 0.1 iota_compare_fusion
  8.7 4.0 %fusion.9 = f32[4,128,384]{2,1,0:T(8,128)S(1)} fusion(bf16[2048,4,384]{2,1,0:T(4,128)(2,1)} %param.14, bf16[128,2048]{1,0:T(8,128)(2,1)} %param.11, f32[2048]{0:T(1024)} %param.13, f32[128]{0:T(128)S(1)} %add_rsqrt_fusion.1), kind=kOutput, calls=%fused_computation.15 | convolution fusion | flops 806354944 | bytes 7610880 | tf_op jit(solution)/shard_map/sd,dhc->hsc/dot_general | solution.py:77
  12.8 0.3 multiply_cosine_fusion
  13.1 0.3 subtract_convert_fusion.1
  13.4 0.1 pad_maximum_fusion
  13.5 17.4 %all_gather.9 = bf16[4,512,128]{2,1,0:T(8,128)(2,1)S(1)} all-gather(bf16[4,128,128]{2,1,0:T(8,128)(2,1)S(1)} %pad_maximum_fusion), channel_id=1, replica_groups=mesh['groups'=2,'ctx'=4,'exp'=4] {'ctx'}, dimensions={1}, use_global_device_ids=true | all-gather | bytes 655360 | tf_op jit(solution)/shard_map/all_gather | solution.py:89
  30.8 0.4 fusion.46
  31.3 0.3 fusion.17
  31.7 17.0 %all_gather.10 = bf16[4,512,128]{2,1,0:T(8,128)(2,1)} all-gather(bf16[4,128,128]{2,1,0:T(8,128)(2,1)S(1)} %slice.74), channel_id=1, replica_groups=mesh['groups'=2,'ctx'=4,'exp'=4] {'ctx'}, dimensions={1}, use_global_device_ids=true | all-gather | bytes 655360 | tf_op jit(solution)/shard_map/all_gather | solution.py:90
  48.6 2.6 %fusion.2 = bf16[128,2048]{1,0:T(8,128)(2,1)} fusion(bf16[4,128,2048]{2,1,0:T(8,128)(2,1)S(1)} %copy-done, bf16[4,512,128]{2,1,0:T(8,128)(2,1)} %all_gather.10, f32[4,128,512]{2,1,0:T(8,128)S(1)} %get-tuple-element.14, f32[4,128]{1,0:T(4,128)S(1)} %is-finite_select_fusion, f32[4,128]{1,0:T(4,128)S(1)} %get-tuple-element.10, f32[4,128]{1,0:T(4,128)S(1)} %get-tuple-element.9), kind=kOutput, calls=%fused_computation.3 | convolution fusion | flops 336527360 | bytes 4200448 | tf_op jit(solution)/shard_map/hsc,hcd->sd/dot_general | solution.py:99
  51.3 0.1 copy.38
  51.4 0.1 eq.35
  51.6 1.2 reduce-window.6
  52.9 0.1 copy.41
  53.0 0.1 copy.42
  53.2 0.1 reduce_sum.59
  53.4 20.1 %reduce-scatter.3.cloned.1.call-done = bf16[32,2048]{1,0:T(8,128)(2,1)} async-done(((bf16[128,2048]{1,0:T(8,128)(2,1)}), bf16[32,2048]{1,0:T(8,128)(2,1)}) %reduce-scatter.3.cloned.1.call-update) | async-done | bytes 131088 | tf_op jit(solution)/shard_map/reduce_scatter | solution.py:98
  73.5 1.1 multiply_reduce_fusion
  74.7 1.2 convolution_convert_fusion
  76.0 12.6 %all_to_all.10 = bf16[16,6,512]{2,1,0:T(8,128)(2,1)S(1)} all-to-all(bf16[16,6,512]{2,1,0:T(8,128)(2,1)S(1)} %bitcast.39), channel_id=1, replica_groups=mesh['groups'=2,'ctx'=4,'exp'=4] {'ctx','exp'}, dimensions={0} | all-to-all | bytes 196608 | tf_op jit(solution)/shard_map/all_to_all | solution.py:130
  88.6 2.6 %fusion.4 = f32[96,1536]{1,0:T(8,128)} fusion(bf16[96,512]{1,0:T(8,128)(2,1)S(1)} %reshape.161, bf16[512,768]{1,0:T(8,128)(2,1)} %bitcast.45, bf16[512,768]{1,0:T(8,128)(2,1)} %bitcast.46), kind=kOutput, calls=%fused_computation.7 | convolution fusion | flops 154140672 | bytes 2260992 | tf_op jit(solution)/shard_map/dot_general | solution.py:138
  91.2 19.7 %reduce-scatter.5.cloned.1.call-done = f32[24,1536]{1,0:T(8,128)} async-done(((f32[96,1536]{1,0:T(8,128)}), f32[24,1536]{1,0:T(8,128)}) %reduce-scatter.5.cloned.1.call-update) | async-done | bytes 147472 | tf_op jit(solution)/shard_map/reduce_scatter | solution.py:143
  110.9 1.0 fusion.36
  111.9 13.4 %all_gather.11 = bf16[96,768]{1,0:T(8,128)(2,1)S(1)} all-gather(bf16[24,768]{1,0:T(8,128)(2,1)S(1)} %fusion.36), channel_id=1, replica_groups=mesh['groups'=2,'ctx'=4,'exp'=4] {'ctx'}, dimensions={0}, use_global_device_ids=true | all-gather | bytes 184320 | tf_op jit(solution)/shard_map/all_gather | solution.py:149
  125.3 0.3 convolution_convert_fusion.1
  125.5 0.7 reshape.162
  126.2 3.5 %all-to-all-start.1 = ((bf16[16,6,512]{2,1,0:T(8,128)(2,1)}), bf16[16,6,512]{2,1,0:T(8,128)(2,1)S(1)}, u32[]{:S(2)}, u32[]{:S(2)}) async-start(bf16[16,6,512]{2,1,0:T(8,128)(2,1)} %reshape.162), calls=%async_computation.3 | async-start | bytes 262144 | tf_op jit(solution)/shard_map/all_to_all | solution.py:153
  129.8 7.9 %all-to-all-done.1 = bf16[16,6,512]{2,1,0:T(8,128)(2,1)S(1)} async-done(((bf16[16,6,512]{2,1,0:T(8,128)(2,1)}), bf16[16,6,512]{2,1,0:T(8,128)(2,1)S(1)}, u32[]{:S(2)}, u32[]{:S(2)}) %all-to-all-start.1) | async-done | bytes 98336 | tf_op jit(solution)/shard_map/all_to_all | solution.py:153
  137.7 0.1 copy.46
  137.8 1.9 %fusion.3 = bf16[32,2048]{1,0:T(8,128)(2,1)} fusion(f32[32,24]{0,1:T(8,128)S(1)} %select_reduce_fusion, bf16[24,2048]{1,0:T(8,128)(2,1)S(1)} %bitcast.42, bf16[32,2048]{1,0:T(8,128)(2,1)S(1)} %copy-done.1, bf16[128,2048]{1,0:T(8,128)(2,1)} %param.11, s32[]{:T(128)S(6)} %select_n.31), kind=kOutput, calls=%fused_computation.5 | convolution fusion | flops 19202048 | bytes 494596 | tf_op jit(solution)/shard_map/dot_general | solution.py:161
  (41 shorter events, 0.7 us)
Async XLA Ops:
  6.5 42.1 %copy-start = (bf16[4,128,2048]{2,1,0:T(8,128)(2,1)S(1)}, bf16[4,128,2048]{2,1,0:T(8,128)(2,1)}, u32[]{:S(2)}) copy-start(bf16[4,128,2048]{2,1,0:T(8,128)(2,1)} %param.15) | copy-start | bytes 6291460
  6.5 67.0 %reduce-scatter.3.cloned.1.call-start = ((), (), s32[]{:S(2)}) async-start(), calls=%async_computation.4 | async-start | bytes 655360 | tf_op jit(solution)/shard_map/reduce_scatter | solution.py:98
  31.3 20.0 %copy-start.4 = (s32[32,6]{0,1:T(8,128)S(1)}, s32[32,6]{0,1:T(8,128)}, u32[]{:S(2)}) copy-start(s32[32,6]{0,1:T(8,128)} %param.17) | copy-start | bytes 2308
  31.6 43.0 %copy-start.3 = (f32[2048]{0:T(1024)S(1)}, f32[2048]{0:T(1024)}, u32[]{:S(2)}) copy-start(f32[2048]{0:T(1024)} %param.16) | copy-start | bytes 24580
  51.2 74.0 %copy-start.2 = (bf16[1,768,512]{2,1,0:T(8,128)(2,1)S(1)}, bf16[1,768,512]{2,1,0:T(8,128)(2,1)}, u32[]{:S(2)}) copy-start(bf16[1,768,512]{2,1,0:T(8,128)(2,1)} %param.21) | copy-start | bytes 2359300
  51.3 59.7 %reduce-scatter.5.cloned.1.call-start = ((), (), s32[]{:S(2)}) async-start(), calls=%async_computation.5 | async-start | bytes 737280 | tf_op jit(solution)/shard_map/reduce_scatter | solution.py:143
  75.9 53.9 %copy-start.5 = (f32[32,6]{0,1:T(8,128)S(1)}, f32[32,6]{0,1:T(8,128)}, u32[]{:S(2)}) copy-start(f32[32,6]{0,1:T(8,128)} %param.18) | copy-start | bytes 2308
  76.0 61.8 %copy-start.1 = (bf16[32,2048]{1,0:T(8,128)(2,1)S(1)}, bf16[32,2048]{1,0:T(8,128)(2,1)}, u32[]{:S(2)}) copy-start(bf16[32,2048]{1,0:T(8,128)(2,1)} %reduce-scatter.3.cloned.1.call-done) | copy-start | bytes 393220
  126.2 11.4 %all-to-all-start.1 = ((bf16[16,6,512]{2,1,0:T(8,128)(2,1)}), bf16[16,6,512]{2,1,0:T(8,128)(2,1)S(1)}, u32[]{:S(2)}, u32[]{:S(2)}) async-start(bf16[16,6,512]{2,1,0:T(8,128)(2,1)} %reshape.162), calls=%async_computation.3 | async-start | bytes 262144 | tf_op jit(solution)/shard_map/all_to_all | solution.py:153
Sparse Core Ops, SparseCore 0:
  51.4 22.1 reduce-scatter.2
  91.3 19.5 reduce-scatter.4

commit v2 on v0

v2 whole, which is shorter than its diff:
```python
import functools

import jax
import jax.numpy as jnp
from jax import lax
from jax.experimental import pallas as pl
from jax.experimental.pallas import tpu as pltpu
from jax.sharding import PartitionSpec as P

CAP = 6
ROWS = 8


epsilon = 1e-06


def rms_norm(rows, gain):
    rows = rows.astype(jnp.float32)
    return rows * lax.rsqrt(jnp.mean(rows * rows, axis=-1, keepdims=True) + epsilon) * gain


def rotary_tables(positions, width):
    freqs = 10000.0 ** (-jnp.arange(width // 2, dtype=jnp.float32) * 2.0 / width)
    angles = positions.astype(jnp.float32)[:, None] * freqs[None, :]
    return (jnp.cos(angles), jnp.sin(angles))


def rotate(vectors, cosines, sines):
    half = vectors.shape[-1] // 2
    first = vectors[..., :half]
    second = vectors[..., half:]
    return jnp.concatenate(
        [first * cosines - second * sines, second * cosines + first * sines], axis=-1
    )


def layer_kernel(
    n_ctx,
    n_exp,
    pieces,
    q_ref,
    kv_ref,
    tokens_ref,
    gain_ref,
    send_matrix_ref,
    combine_ref,
    w_out_hbm,
    w_gate_hbm,
    w_up_hbm,
    w_down_hbm,
    out_ref,
    kv_buf,
    peak_ref,
    total_ref,
    sum_ref,
    attended_ref,
    w_out,
    w_gate,
    w_up,
    w_down,
    rs_send,
    rs_recv,
    rows_send,
    rows_recv,
    part_send,
    part_recv,
    hidden_ref,
    back_send,
    back_recv,
    weight_sem,
    kv_send_sem,
    kv_recv_sem,
    rs_send_sem,
    rs_recv_sem,
    rows_send_sem,
    rows_recv_sem,
    part_send_sem,
    part_recv_sem,
    hidden_send_sem,
    hidden_recv_sem,
    back_send_sem,
    back_recv_sem,
):
    f32 = jnp.float32
    bf16 = jnp.bfloat16
    devices = n_ctx * n_exp
    c = lax.axis_index("ctx")
    e = lax.axis_index("exp")
    me = c * n_exp + e
    heads, seq, head_dim = q_ref.shape
    own, width = tokens_ref.shape
    columns = width // n_ctx
    piece = columns // pieces
    hidden_width = w_gate.shape[1]

    loads = [
        pltpu.make_async_copy(w_out_hbm, w_out, weight_sem.at[0]),
        pltpu.make_async_copy(w_gate_hbm, w_gate, weight_sem.at[1]),
        pltpu.make_async_copy(w_up_hbm, w_up, weight_sem.at[2]),
        pltpu.make_async_copy(w_down_hbm, w_down, weight_sem.at[3]),
    ]
    for load in loads:
        load.start()

    barrier = pltpu.get_barrier_semaphore()

    def greet(k, carry):
        peer = lax.rem(me + k, devices)
        pl.semaphore_signal(
            barrier,
            inc=1,
            device_id={"ctx": peer // n_exp, "exp": lax.rem(peer, n_exp)},
            device_id_type=pl.DeviceIdType.MESH,
        )
        return carry

    lax.fori_loop(1, devices, greet, 0)
    pl.semaphore_wait(barrier, devices - 1)

    def remote(src, dst, send_sem, recv_sem, device):
        return pltpu.make_async_remote_copy(
            src_ref=src,
            dst_ref=dst,
            send_sem=send_sem,
            recv_sem=recv_sem,
            device_id=device,
            device_id_type=pl.DeviceIdType.MESH,
        )

    def hop(source, block):
        return remote(
            source,
            kv_buf.at[block],
            kv_send_sem.at[block],
            kv_recv_sem.at[block],
            {"ctx": lax.rem(c + 1, n_ctx)},
        )

    @pl.when(c + 1 < n_ctx)
    def _():
        hop(kv_ref, c).start()

    scale = head_dim ** (-0.5)
    over_last = (((1,), (1,)), ((), ()))
    allowed = lax.broadcasted_iota(jnp.int32, (seq, seq), 1) <= lax.broadcasted_iota(
        jnp.int32, (seq, seq), 0
    )
    for head in range(heads):
        scores = (
            lax.dot_general(q_ref[head], kv_ref[head], over_last, preferred_element_type=f32)
            * scale
        )
        scores = jnp.where(allowed, scores, -jnp.inf)
        peak = jnp.max(scores, axis=1, keepdims=True)
        probs = jnp.exp(scores - peak)
        peak_ref[head] = peak
        total_ref[head] = jnp.sum(probs, axis=1, keepdims=True)
        sum_ref[head] = jnp.dot(
            probs.astype(bf16), kv_ref[heads + head], preferred_element_type=f32
        )

    def earlier_block(step, carry):
        @pl.when(step <= c)
        def _():
            block = c - step
            hop(kv_buf.at[block], block).wait_recv()

            @pl.when(c + 1 < n_ctx)
            def _():
                hop(kv_buf.at[block], block).start()

            for head in range(heads):
                scores = (
                    lax.dot_general(
                        q_ref[head], kv_buf[block, head], over_last, preferred_element_type=f32
                    )
                    * scale
                )
                old_peak = peak_ref[head]
                peak = jnp.maximum(old_peak, jnp.max(scores, axis=1, keepdims=True))
                probs = jnp.exp(scores - peak)
                factor = jnp.exp(old_peak - peak)
                peak_ref[head] = peak
                total_ref[head] = total_ref[head] * factor + jnp.sum(probs, axis=1, keepdims=True)
                sum_ref[head] = sum_ref[head] * factor + jnp.dot(
                    probs.astype(bf16), kv_buf[block, heads + head], preferred_element_type=f32
                )

        return carry

    lax.fori_loop(1, n_ctx, earlier_block, 0)
    for head in range(heads):
        attended_ref[:, head * head_dim : (head + 1) * head_dim] = (
            sum_ref[head] / total_ref[head]
        ).astype(bf16)

    loads[0].wait()
    chunk = 512
    for start in range(0, width, chunk):
        part = jnp.dot(
            attended_ref[...], w_out[:, start : start + chunk], preferred_element_type=f32
        )
        rs_send[:, :, start : start + chunk] = part.astype(bf16).reshape(n_exp, own, chunk)

    def share(k):
        peer = lax.rem(e + k, n_exp)
        return remote(
            rs_send.at[peer],
            rs_recv.at[k],
            rs_send_sem.at[k],
            rs_recv_sem.at[k],
            {"exp": peer},
        )

    def start_of(copy_of):
        def step(k, carry):
            copy_of(k).start()
            return carry

        return step

    def wait_recv_of(copy_of):
        def step(k, carry):
            copy_of(k).wait_recv()
            return carry

        return step

    def wait_send_of(copy_of):
        def step(k, carry):
            copy_of(k).wait_send()
            return carry

        return step

    lax.fori_loop(1, n_exp, start_of(share), 0)
    residual = tokens_ref[...].astype(f32) + rs_send[e].astype(f32)
    lax.fori_loop(1, n_exp, wait_recv_of(share), 0)
    for k in range(1, n_exp):
        residual = residual + rs_recv[k].astype(f32)

    square = jnp.mean(residual * residual, axis=-1, keepdims=True)
    normed = (residual * lax.rsqrt(square + epsilon) * gain_ref[...]).astype(bf16)
    outgoing = jnp.dot(send_matrix_ref[...], normed, preferred_element_type=f32)

    def packed(rows):
        parts = [
            rows[:, p * piece : (p + 1) * piece].reshape(-1, ROWS, piece) for p in range(pieces)
        ]
        if pieces == 1:
            parts.append(jnp.zeros_like(parts[0]))
        return jnp.concatenate(parts, axis=1).astype(bf16)

    def unpacked(rows, p):
        return rows[:, p * ROWS : (p + 1) * ROWS, :].reshape(-1, piece)

    for block in range(n_ctx):
        rows_send[block * n_exp : (block + 1) * n_exp] = packed(
            outgoing[:, block * columns : (block + 1) * columns]
        )

    def to_all(send, recv, send_sem, recv_sem):
        def copy_of(k):
            peer = lax.rem(me + k, devices)
            return remote(
                send.at[peer],
                recv.at[me],
                send_sem.at[k],
                recv_sem.at[k],
                {"ctx": peer // n_exp, "exp": lax.rem(peer, n_exp)},
            )

        return copy_of

    dispatch = to_all(rows_send, rows_recv, rows_send_sem, rows_recv_sem)
    lax.fori_loop(1, devices, start_of(dispatch), 0)
    rows_recv[me] = rows_send[me]
    loads[1].wait()
    loads[2].wait()
    lax.fori_loop(1, devices, wait_recv_of(dispatch), 0)
    incoming = rows_recv[...].astype(f32)
    gate = None
    for p in range(pieces):
        rows = unpacked(incoming, p).astype(bf16)
        gate_p = jnp.dot(
            rows, w_gate[p * piece : (p + 1) * piece, :], preferred_element_type=f32
        )
        up_p = jnp.dot(rows, w_up[p * piece : (p + 1) * piece, :], preferred_element_type=f32)
        gate, up = (gate_p, up_p) if gate is None else (gate + gate_p, up + up_p)
    part_send[:, :, :hidden_width] = gate.astype(bf16).reshape(n_ctx, -1, hidden_width)
    part_send[:, :, hidden_width:] = up.astype(bf16).reshape(n_ctx, -1, hidden_width)

    def partial(k):
        peer = lax.rem(c + k, n_ctx)
        return remote(
            part_send.at[peer],
            part_recv.at[k],
            part_send_sem.at[k],
            part_recv_sem.at[k],
            {"ctx": peer},
        )

    lax.fori_loop(1, n_ctx, start_of(partial), 0)
    summed = part_send[c].astype(f32)
    lax.fori_loop(1, n_ctx, wait_recv_of(partial), 0)
    for k in range(1, n_ctx):
        summed = summed + part_recv[k].astype(f32)
    gate = summed[:, :hidden_width]
    hidden_ref[c] = (gate / (1.0 + jnp.exp(-gate)) * summed[:, hidden_width:]).astype(bf16)

    def hidden_copy(k):
        return remote(
            hidden_ref.at[c],
            hidden_ref.at[c],
            hidden_send_sem.at[k],
            hidden_recv_sem.at[k],
            {"ctx": lax.rem(c + k, n_ctx)},
        )

    lax.fori_loop(1, n_ctx, start_of(hidden_copy), 0)
    loads[3].wait()
    lax.fori_loop(1, n_ctx, wait_recv_of(hidden_copy), 0)
    expert_out = jnp.dot(
        hidden_ref[...].reshape(-1, hidden_width), w_down[...], preferred_element_type=f32
    )
    back_send[...] = packed(expert_out)
    back = to_all(back_send, back_recv, back_send_sem, back_recv_sem)
    lax.fori_loop(1, devices, start_of(back), 0)
    back_recv[me] = back_send[me]
    lax.fori_loop(1, devices, wait_recv_of(back), 0)
    for block in range(n_ctx):
        rows = back_recv[block * n_exp : (block + 1) * n_exp].astype(f32)
        for p in range(pieces):
            begin = block * columns + p * piece
            mixed = jnp.dot(
                combine_ref[...],
                unpacked(rows, p),
                precision=lax.Precision.HIGHEST,
                preferred_element_type=f32,
            )
            out_ref[:, begin : begin + piece] = (
                residual[:, begin : begin + piece] + mixed
            ).astype(bf16)

    def sent_block(step, carry):
        @pl.when(jnp.logical_and(step <= c, c + 1 < n_ctx))
        def _():
            hop(kv_buf.at[c - step], c - step).wait_send()

        return carry

    lax.fori_loop(0, n_ctx, sent_block, 0)
    lax.fori_loop(1, n_exp, wait_send_of(share), 0)
    lax.fori_loop(1, devices, wait_send_of(dispatch), 0)
    lax.fori_loop(1, n_ctx, wait_send_of(partial), 0)
    lax.fori_loop(1, n_ctx, wait_send_of(hidden_copy), 0)
    lax.fori_loop(1, devices, wait_send_of(back), 0)


def body(
    tokens,
    positions,
    attn_gain,
    w_qkv,
    w_out,
    moe_gain,
    expert_ids,
    gate_probs,
    w_gate,
    w_up,
    w_down,
):
    seq_dev = tokens.shape[0]
    width = tokens.shape[1]
    head_dim = w_out.shape[1]
    heads_here = w_out.shape[0]
    n_ctx = lax.axis_size("ctx")
    n_exp = lax.axis_size("exp")
    devices = n_ctx * n_exp
    normed = rms_norm(tokens, attn_gain).astype(jnp.bfloat16)
    projected = jnp.einsum("sd,dhc->hsc", normed, w_qkv, preferred_element_type=jnp.float32)
    cosines, sines = rotary_tables(positions, head_dim)
    queries = rotate(projected[..., :head_dim], cosines, sines).astype(jnp.bfloat16)
    key_rows = rotate(projected[..., head_dim : 2 * head_dim], cosines, sines).astype(jnp.bfloat16)
    value_rows = projected[..., 2 * head_dim :].astype(jnp.bfloat16)
    keys_values = jnp.concatenate([key_rows, value_rows], axis=0)
    own = seq_dev // n_exp
    own_tokens = lax.dynamic_slice_in_dim(tokens, lax.axis_index("exp") * own, own, 0)

    flight = n_exp
    hits = expert_ids[:, :, None] == jnp.arange(flight, dtype=jnp.int32)[None, None, :]
    marks = jnp.any(hits, axis=1)
    weight = jnp.sum(jnp.where(hits, gate_probs[:, :, None], 0.0), axis=1)
    before = jnp.arange(own)[:, None] > jnp.arange(own)[None, :]
    place = jnp.sum((before[:, :, None] & marks[None, :, :]).astype(jnp.int32), axis=1)
    in_slot = marks[:, :, None] & (
        place[:, :, None] == jnp.arange(ROWS, dtype=jnp.int32)[None, None, :]
    )
    send_matrix = in_slot.reshape(own, flight * ROWS).T.astype(jnp.bfloat16)
    combine = jnp.where(in_slot, weight[:, :, None], 0.0).reshape(own, flight * ROWS)

    columns = width // n_ctx
    pieces = 2 if columns % 256 == 0 else 1
    piece = columns // pieces
    hidden_width = w_gate.shape[2]
    bf16 = jnp.bfloat16
    vmem = pl.BlockSpec(memory_space=pltpu.VMEM)
    anywhere = pl.BlockSpec(memory_space=pl.ANY)
    dma = pltpu.SemaphoreType.DMA
    return pl.pallas_call(
        functools.partial(layer_kernel, n_ctx, n_exp, pieces),
        out_shape=jax.ShapeDtypeStruct((own, width), bf16),
        in_specs=[vmem] * 6 + [anywhere] * 4,
        out_specs=vmem,
        scratch_shapes=[
            pltpu.VMEM((n_ctx, 2 * heads_here, seq_dev, head_dim), bf16),
            pltpu.VMEM((heads_here, seq_dev, 1), jnp.float32),
            pltpu.VMEM((heads_here, seq_dev, 1), jnp.float32),
            pltpu.VMEM((heads_here, seq_dev, head_dim), jnp.float32),
            pltpu.VMEM((seq_dev, heads_here * head_dim), bf16),
            pltpu.VMEM((heads_here * head_dim, width), bf16),
            pltpu.VMEM(w_gate.shape[1:], bf16),
            pltpu.VMEM(w_up.shape[1:], bf16),
            pltpu.VMEM(w_down.shape[1:], bf16),
            pltpu.VMEM((n_exp, own, width), bf16),
            pltpu.VMEM((n_exp, own, width), bf16),
            pltpu.VMEM((devices, 2 * ROWS, piece), bf16),
            pltpu.VMEM((devices, 2 * ROWS, piece), bf16),
            pltpu.VMEM((n_ctx, n_exp * ROWS, 2 * hidden_width), bf16),
            pltpu.VMEM((n_ctx, n_exp * ROWS, 2 * hidden_width), bf16),
            pltpu.VMEM((n_ctx, n_exp * ROWS, hidden_width), bf16),
            pltpu.VMEM((devices, 2 * ROWS, piece), bf16),
            pltpu.VMEM((devices, 2 * ROWS, piece), bf16),
            dma((4,)),
            dma((n_ctx,)),
            dma((n_ctx,)),
            dma((n_exp,)),
            dma((n_exp,)),
            dma((devices,)),
            dma((devices,)),
            dma((n_ctx,)),
            dma((n_ctx,)),
            dma((n_ctx,)),
            dma((n_ctx,)),
            dma((devices,)),
            dma((devices,)),
        ],
        compiler_params=pltpu.CompilerParams(
            collective_id=0, has_side_effects=True, vmem_limit_bytes=60 * 1024 * 1024
        ),
    )(
        queries,
        keys_values,
        own_tokens,
        moe_gain.reshape(1, width),
        send_matrix,
        combine,
        w_out.reshape(heads_here * head_dim, width),
        w_gate[0],
        w_up[0],
        w_down[0],
    )


def solution(mesh):
    return jax.shard_map(
        body,
        mesh=mesh,
        in_specs=(
            P(("groups", "ctx"), None),
            P(("groups", "ctx")),
            P(),
            P(None, "exp", None),
            P("exp", None, None),
            P(),
            P(("groups", "ctx", "exp"), None),
            P(("groups", "ctx", "exp"), None),
            P("exp", "ctx", None),
            P("exp", "ctx", None),
            P("exp", None, "ctx"),
        ),
        out_specs=P(("groups", "ctx", "exp"), None),
        check_vma=False,
    )
```

time: 268 us -> 77.5 us (0.29)
  waiting for transfers between devices: 183 us -> 0 us
  Pallas kernels: 0 us -> 64.8 us
  blocking collectives: 42 us -> 0 us
  between operations: 15.2 us -> 0.11 us
  matrix products: 16.6 us -> 4.05 us
  starting transfers between devices: 3.45 us -> 0 us
    all_gather x3 -> x0, waiting for transfers between devices: 159 us -> none  [the longest x1 63.4 us: body(): lax.all_gather(w_down, 'ctx', axis=2, tiled=True)[0]]
    pallas_call x0 -> x1, Pallas kernels: none -> 64.8 us  [body(): pl.pallas_call(functools.partial(layer_kernel, n_ctx, n_exp, pieces), out...]
    all_gather x2 -> x0, blocking collectives: 35 us -> none  [the longest x1 18 us: body(): lax.all_gather(key_rows, 'ctx', axis=1, tiled=True)]
    reduce_scatter x1 -> x0, waiting for transfers between devices: 18.5 us -> none  [body(): lax.psum_scatter(jnp.einsum('hsc,hcd->sd', attended, w_out, preferred_ele...]
    dot_general x6 -> x0, matrix products: 12.6 us -> none  [the longest x1 3.98 us: body(): jnp.dot(hidden, lax.all_gather(w_down, 'ctx', axis=2, tiled=True)[0], pre...]
    all_to_all x1 -> x0, blocking collectives: 7.02 us -> none  [body(): lax.all_to_all(outgoing.reshape(flight, CAP, width), 'exp', split_axis=0,...]
    all_to_all x1 -> x0, waiting for transfers between devices: 4.56 us -> none  [body(): lax.all_to_all(expert_out.reshape(flight, CAP, width), 'exp', split_axis=...]
    all_to_all x1 -> x0, starting transfers between devices: 3.33 us -> none  [body(): lax.all_to_all(expert_out.reshape(flight, CAP, width), 'exp', split_axis=...]
  transfers between devices with their start and end apart: 5 -> 0, of which waited for: 5 -> 0; matrix products, arithmetic and copies ran while one was open for 3% -> 0% of each run, Pallas kernels for 0% -> 0%
where the time goes in v2:
time: 77.5 us; the launch traced here: 77.3 us
  Pallas kernels  64.8 us (84%)
  other arithmetic  4.2 us (5%)
  local copies, waits for them, and re-layouts  4.19 us (5%)
  matrix products  4.05 us (5%)
    pallas_call x1, Pallas kernels, body(): pl.pallas_call(functools.partial(layer_kernel, n_ctx, n_exp, pieces), out...  64.8 us
    dot_general x1, matrix products, body(): jnp.einsum('sd,dhc->hsc', normed, w_qkv, preferred_element_type=jnp.float32)  4.05 us
    unnamed x7, local copies, waits for them, and re-layouts  1.58 us
    dynamic_slice x1, local copies, waits for them, and re-layouts, body(): lax.dynamic_slice_in_dim(tokens, lax.axis_index('exp') * own, own, 0)  1.57 us

profile of v2, /device:TPU:0, one launch (start us, length us, event | category | flops | bytes accessed | tf_op | source)
XLA Modules:
  0.0 77.3 jit_solution(15470021105943209994)
XLA Ops:
  0.0 0.0 copy-start.2
  0.0 1.2 %fusion.5 = f32[128]{0:T(128)S(1)} fusion(bf16[128,2048]{1,0:T(8,128)(2,1)} %param.11), kind=kLoop, calls=%fused_computation.5 | loop fusion | flops 786304 | bytes 524800 | tf_op jit(solution)/shard_map/reduce_sum | solution.py:19
  1.3 0.0 copy-start
  1.3 0.0 copy-start.1
  1.3 4.0 %fusion.2 = f32[4,128,384]{2,1,0:T(8,128)S(1)} fusion(bf16[2048,4,384]{2,1,0:T(4,128)(2,1)} %param.14, bf16[128,2048]{1,0:T(8,128)(2,1)} %param.11, f32[2048]{0:T(1024)} %param.13, f32[128]{0:T(128)S(1)} %add_rsqrt_fusion), kind=kOutput, calls=%fused_computation.4 | convolution fusion | flops 806354944 | bytes 7610880 | tf_op jit(solution)/shard_map/sd,dhc->hsc/dot_general | solution.py:381
  5.3 0.0 copy-done.2
  5.4 0.3 multiply_cosine_fusion
  5.7 0.3 subtract_convert_fusion
  6.0 0.8 %pad_maximum_fusion.kv_ref = bf16[8,128,128]{2,1,0:T(8,128)(2,1)} fusion(bf16[4,128,128]{2,1,0:T(8,128)(2,1)S(1)} %slice.41, bf16[4,128,64]{2,1,0:T(8,128)(2,1)S(1)} %get-tuple-element.8, bf16[4,128,64]{2,1,0:T(8,128)(2,1)S(1)} %get-tuple-element.7), kind=kLoop, calls=%fused_computation.12 | loop fusion | flops 786432 | bytes 524288 | tf_op jit(solution)/shard_map/concatenate | solution.py:386
  6.8 0.8 pad_maximum_fusion.1.q_ref
  7.5 1.6 %constant_dynamic-slice_fusion.tokens_ref = bf16[32,2048]{1,0:T(8,128)(2,1)} fusion(bf16[128,2048]{1,0:T(8,128)(2,1)} %param.11, s32[]{:T(128)S(6)} %select_n.12), kind=kLoop, calls=%fused_computation.33 | loop fusion | bytes 262148 | tf_op jit(solution)/shard_map/dynamic_slice | solution.py:388
  9.1 0.0 copy-done
  9.1 0.1 convert_reduce_fusion
  9.3 0.1 copy.25
  9.4 0.1 copy.26
  9.5 0.0 copy-done.1
  9.5 0.1 copy.27
  9.6 0.1 eq.40
  9.7 0.6 broadcast_select_fusion
  10.3 0.7 copy.28.send_matrix_ref
  11.0 64.8 %shard_map.109 = bf16[32,2048]{1,0:T(8,128)(2,1)} custom-call(bf16[4,128,128]{2,1,0:T(8,128)(2,1)} %pad_maximum_fusion.1.q_ref, bf16[8,128,128]{2,1,0:T(8,128)(2,1)} %pad_maximum_fusion.kv_ref, bf16[32,2048]{1,0:T(8,128)(2,1)} %constant_dynamic-slice_fusion.tokens_ref, f32[1,2048]{1,0:T(1,128)} %bitcast.22, bf16[32,32]{1,0:T(8,128)(2,1)} %copy.28.send_matrix_ref, ...), custom_call_target="tpu_custom_call" | custom-call | tf_op jit(solution)/shard_map/pallas_call | solution.py:410
  75.8 1.6 %copy.34 = bf16[32,2048]{1,0:T(8,128)(2,1)} copy(bf16[32,2048]{1,0:T(8,128)(2,1)} %shard_map.109) | data formatting | bytes 262144
  (12 shorter events, 0.1 us)
Async XLA Ops:
  0.0 5.3 %copy-start.2 = (s32[128]{0:T(128)S(1)}, s32[128]{0:T(128)}, u32[]{:S(2)}) copy-start(s32[128]{0:T(128)} %param.12) | copy-start | bytes 1540
  1.3 7.9 %copy-start = (s32[32,6]{0,1:T(8,128)S(1)}, s32[32,6]{0,1:T(8,128)}, u32[]{:S(2)}) copy-start(s32[32,6]{0,1:T(8,128)} %param.17) | copy-start | bytes 2308
  1.3 8.2 %copy-start.1 = (f32[32,6]{0,1:T(8,128)S(1)}, f32[32,6]{0,1:T(8,128)}, u32[]{:S(2)}) copy-start(f32[32,6]{0,1:T(8,128)} %param.18) | copy-start | bytes 2308

commit v3 on v2

--- a/solution.py
+++ b/solution.py
@@ -22,24 +22,33 @@
 def rotary_tables(positions, width):
     freqs = 10000.0 ** (-jnp.arange(width // 2, dtype=jnp.float32) * 2.0 / width)
     angles = positions.astype(jnp.float32)[:, None] * freqs[None, :]
-    return (jnp.cos(angles), jnp.sin(angles))
-
-
-def rotate(vectors, cosines, sines):
-    half = vectors.shape[-1] // 2
-    first = vectors[..., :half]
-    second = vectors[..., half:]
-    return jnp.concatenate(
-        [first * cosines - second * sines, second * cosines + first * sines], axis=-1
+    cosines, sines = jnp.cos(angles), jnp.sin(angles)
+    return (
+        jnp.concatenate([cosines, cosines], axis=1),
+        jnp.concatenate([-sines, sines], axis=1),
     )
+
+
+def each(begin, end, step):
+    if end - begin <= 16:
+        for k in range(begin, end):
+            step(k)
+        return
+
+    def one(k, carry):
+        step(k)
+        return carry
+
+    lax.fori_loop(begin, end, one, 0)
 
 
 def layer_kernel(
     n_ctx,
     n_exp,
     pieces,
-    q_ref,
-    kv_ref,
+    projected_ref,
+    cosines_ref,
+    sines_ref,
     tokens_ref,
     gain_ref,
     send_matrix_ref,
@@ -49,6 +58,7 @@
     w_up_hbm,
     w_down_hbm,
     out_ref,
+    q_ref,
     kv_buf,
     peak_ref,
     total_ref,
@@ -88,7 +98,8 @@
     e = lax.axis_index("exp")
     me = c * n_exp + e
     heads, seq, head_dim = q_ref.shape
-    own, width = tokens_ref.shape
+    width = tokens_ref.shape[1]
+    own = seq // n_exp
     columns = width // n_ctx
     piece = columns // pieces
     hidden_width = w_gate.shape[1]
@@ -104,7 +115,7 @@
 
     barrier = pltpu.get_barrier_semaphore()
 
-    def greet(k, carry):
+    def greet(k):
         peer = lax.rem(me + k, devices)
         pl.semaphore_signal(
             barrier,
@@ -112,9 +123,18 @@
             device_id={"ctx": peer // n_exp, "exp": lax.rem(peer, n_exp)},
             device_id_type=pl.DeviceIdType.MESH,
         )
-        return carry
-
-    lax.fori_loop(1, devices, greet, 0)
+
+    each(1, devices, greet)
+
+    def rotated(vectors):
+        return (
+            vectors * cosines_ref[...]
+            + pltpu.roll(vectors, head_dim // 2, axis=1) * sines_ref[...]
+        ).astype(bf16)
+
+    for head in range(heads):
+        kv_buf[c, head] = rotated(projected_ref[head, :, head_dim : 2 * head_dim])
+        kv_buf[c, heads + head] = projected_ref[head, :, 2 * head_dim :].astype(bf16)
     pl.semaphore_wait(barrier, devices - 1)
 
     def remote(src, dst, send_sem, recv_sem, device):
@@ -127,9 +147,9 @@
             device_id_type=pl.DeviceIdType.MESH,
         )
 
-    def hop(source, block):
+    def hop(block):
         return remote(
-            source,
+            kv_buf.at[block],
             kv_buf.at[block],
             kv_send_sem.at[block],
             kv_recv_sem.at[block],
@@ -138,7 +158,7 @@
 
     @pl.when(c + 1 < n_ctx)
     def _():
-        hop(kv_ref, c).start()
+        hop(c).start()
 
     scale = head_dim ** (-0.5)
     over_last = (((1,), (1,)), ((), ()))
@@ -146,8 +166,9 @@
         jnp.int32, (seq, seq), 0
     )
     for head in range(heads):
+        q_ref[head] = rotated(projected_ref[head, :, :head_dim])
         scores = (
-            lax.dot_general(q_ref[head], kv_ref[head], over_last, preferred_element_type=f32)
+            lax.dot_general(q_ref[head], kv_buf[c, head], over_last, preferred_element_type=f32)
             * scale
         )
         scores = jnp.where(allowed, scores, -jnp.inf)
@@ -156,18 +177,18 @@
         peak_ref[head] = peak
         total_ref[head] = jnp.sum(probs, axis=1, keepdims=True)
         sum_ref[head] = jnp.dot(
-            probs.astype(bf16), kv_ref[heads + head], preferred_element_type=f32
+            probs.astype(bf16), kv_buf[c, heads + head], preferred_element_type=f32
         )
 
     def earlier_block(step, carry):
         @pl.when(step <= c)
         def _():
             block = c - step
-            hop(kv_buf.at[block], block).wait_recv()
+            hop(block).wait_recv()
 
             @pl.when(c + 1 < n_ctx)
             def _():
-                hop(kv_buf.at[block], block).start()
+                hop(block).start()
 
             for head in range(heads):
                 scores = (
@@ -213,29 +234,17 @@
         )
 
     def start_of(copy_of):
-        def step(k, carry):
-            copy_of(k).start()
-            return carry
-
-        return step
+        return lambda k: copy_of(k).start()
 
     def wait_recv_of(copy_of):
-        def step(k, carry):
-            copy_of(k).wait_recv()
-            return carry
-
-        return step
+        return lambda k: copy_of(k).wait_recv()
 
     def wait_send_of(copy_of):
-        def step(k, carry):
-            copy_of(k).wait_send()
-            return carry
-
-        return step
-
-    lax.fori_loop(1, n_exp, start_of(share), 0)
-    residual = tokens_ref[...].astype(f32) + rs_send[e].astype(f32)
-    lax.fori_loop(1, n_exp, wait_recv_of(share), 0)
+        return lambda k: copy_of(k).wait_send()
+
+    each(1, n_exp, start_of(share))
+    residual = tokens_ref[pl.ds(pl.multiple_of(e * own, own), own), :].astype(f32) + rs_send[e].astype(f32)
+    each(1, n_exp, wait_recv_of(share))
     for k in range(1, n_exp):
         residual = residual + rs_recv[k].astype(f32)
 
@@ -273,22 +282,41 @@
         return copy_of
 
     dispatch = to_all(rows_send, rows_recv, rows_send_sem, rows_recv_sem)
-    lax.fori_loop(1, devices, start_of(dispatch), 0)
+    each(1, devices, start_of(dispatch))
     rows_recv[me] = rows_send[me]
     loads[1].wait()
     loads[2].wait()
-    lax.fori_loop(1, devices, wait_recv_of(dispatch), 0)
-    incoming = rows_recv[...].astype(f32)
+    each(1, devices, wait_recv_of(dispatch))
+    used = n_exp * CAP
+    slot = lax.broadcasted_iota(jnp.int32, (used, n_exp * ROWS), 1)
+    place = lax.rem(slot, ROWS)
+    keep = jnp.logical_and(
+        lax.broadcasted_iota(jnp.int32, slot.shape, 0) == (slot // ROWS) * CAP + place, place < CAP
+    )
+    keep = keep.astype(f32).astype(bf16)
     gate = None
     for p in range(pieces):
-        rows = unpacked(incoming, p).astype(bf16)
+        rows = jnp.concatenate(
+            [
+                jnp.dot(
+                    keep,
+                    unpacked(
+                        rows_recv[block * n_exp : (block + 1) * n_exp].astype(f32), p
+                    ).astype(bf16),
+                    preferred_element_type=f32,
+                )
+                for block in range(n_ctx)
+            ],
+            axis=0,
+        ).astype(bf16)
         gate_p = jnp.dot(
             rows, w_gate[p * piece : (p + 1) * piece, :], preferred_element_type=f32
         )
         up_p = jnp.dot(rows, w_up[p * piece : (p + 1) * piece, :], preferred_element_type=f32)
         gate, up = (gate_p, up_p) if gate is None else (gate + gate_p, up + up_p)
-    part_send[:, :, :hidden_width] = gate.astype(bf16).reshape(n_ctx, -1, hidden_width)
-    part_send[:, :, hidden_width:] = up.astype(bf16).reshape(n_ctx, -1, hidden_width)
+    for block in range(n_ctx):
+        mine = slice(block * used, (block + 1) * used)
+        part_send[block] = jnp.concatenate([gate[mine], up[mine]], axis=0).astype(bf16)
 
     def partial(k):
         peer = lax.rem(c + k, n_ctx)
@@ -300,13 +328,15 @@
             {"ctx": peer},
         )
 
-    lax.fori_loop(1, n_ctx, start_of(partial), 0)
+    each(1, n_ctx, start_of(partial))
     summed = part_send[c].astype(f32)
-    lax.fori_loop(1, n_ctx, wait_recv_of(partial), 0)
+    each(1, n_ctx, wait_recv_of(partial))
     for k in range(1, n_ctx):
         summed = summed + part_recv[k].astype(f32)
-    gate = summed[:, :hidden_width]
-    hidden_ref[c] = (gate / (1.0 + jnp.exp(-gate)) * summed[:, hidden_width:]).astype(bf16)
+    gate = summed[:used]
+    hidden = gate / (1.0 + jnp.exp(-gate)) * summed[used:]
+    half = hidden_width // 2
+    hidden_ref[c] = jnp.concatenate([hidden[:, :half], hidden[:, half:]], axis=0).astype(bf16)
 
     def hidden_copy(k):
         return remote(
@@ -317,17 +347,23 @@
             {"ctx": lax.rem(c + k, n_ctx)},
         )
 
-    lax.fori_loop(1, n_ctx, start_of(hidden_copy), 0)
+    each(1, n_ctx, start_of(hidden_copy))
     loads[3].wait()
-    lax.fori_loop(1, n_ctx, wait_recv_of(hidden_copy), 0)
-    expert_out = jnp.dot(
-        hidden_ref[...].reshape(-1, hidden_width), w_down[...], preferred_element_type=f32
-    )
-    back_send[...] = packed(expert_out)
+    each(1, n_ctx, wait_recv_of(hidden_copy))
+    hidden = hidden_ref[...].astype(f32)
+    expert_out = None
+    for p in range(2):
+        rows = hidden[:, p * used : (p + 1) * used, :].reshape(-1, half).astype(bf16)
+        out_p = jnp.dot(rows, w_down[p * half : (p + 1) * half, :], preferred_element_type=f32)
+        expert_out = out_p if expert_out is None else expert_out + out_p
+    for block in range(n_ctx):
+        rows = expert_out[block * used : (block + 1) * used].astype(bf16)
+        rows = lax.dot_general(keep, rows, (((0,), (0,)), ((), ())), preferred_element_type=f32)
+        back_send[block * n_exp : (block + 1) * n_exp] = packed(rows)
     back = to_all(back_send, back_recv, back_send_sem, back_recv_sem)
-    lax.fori_loop(1, devices, start_of(back), 0)
+    each(1, devices, start_of(back))
     back_recv[me] = back_send[me]
-    lax.fori_loop(1, devices, wait_recv_of(back), 0)
+    each(1, devices, wait_recv_of(back))
     for block in range(n_ctx):
         rows = back_recv[block * n_exp : (block + 1) * n_exp].astype(f32)
         for p in range(pieces):
@@ -345,16 +381,16 @@
     def sent_block(step, carry):
         @pl.when(jnp.logical_and(step <= c, c + 1 < n_ctx))
         def _():
-            hop(kv_buf.at[c - step], c - step).wait_send()
+            hop(c - step).wait_send()
 
         return carry
 
     lax.fori_loop(0, n_ctx, sent_block, 0)
-    lax.fori_loop(1, n_exp, wait_send_of(share), 0)
-    lax.fori_loop(1, devices, wait_send_of(dispatch), 0)
-    lax.fori_loop(1, n_ctx, wait_send_of(partial), 0)
-    lax.fori_loop(1, n_ctx, wait_send_of(hidden_copy), 0)
-    lax.fori_loop(1, devices, wait_send_of(back), 0)
+    each(1, n_exp, wait_send_of(share))
+    each(1, devices, wait_send_of(dispatch))
+    each(1, n_ctx, wait_send_of(partial))
+    each(1, n_ctx, wait_send_of(hidden_copy))
+    each(1, devices, wait_send_of(back))
 
 
 def body(
@@ -380,12 +416,7 @@
     normed = rms_norm(tokens, attn_gain).astype(jnp.bfloat16)
     projected = jnp.einsum("sd,dhc->hsc", normed, w_qkv, preferred_element_type=jnp.float32)
     cosines, sines = rotary_tables(positions, head_dim)
-    queries = rotate(projected[..., :head_dim], cosines, sines).astype(jnp.bfloat16)
-    key_rows = rotate(projected[..., head_dim : 2 * head_dim], cosines, sines).astype(jnp.bfloat16)
-    value_rows = projected[..., 2 * head_dim :].astype(jnp.bfloat16)
-    keys_values = jnp.concatenate([key_rows, value_rows], axis=0)
     own = seq_dev // n_exp
-    own_tokens = lax.dynamic_slice_in_dim(tokens, lax.axis_index("exp") * own, own, 0)
 
     flight = n_exp
     hits = expert_ids[:, :, None] == jnp.arange(flight, dtype=jnp.int32)[None, None, :]
@@ -410,9 +441,10 @@
     return pl.pallas_call(
         functools.partial(layer_kernel, n_ctx, n_exp, pieces),
         out_shape=jax.ShapeDtypeStruct((own, width), bf16),
-        in_specs=[vmem] * 6 + [anywhere] * 4,
+        in_specs=[vmem] * 7 + [anywhere] * 4,
         out_specs=vmem,
         scratch_shapes=[
+            pltpu.VMEM((heads_here, seq_dev, head_dim), bf16),
             pltpu.VMEM((n_ctx, 2 * heads_here, seq_dev, head_dim), bf16),
             pltpu.VMEM((heads_here, seq_dev, 1), jnp.float32),
             pltpu.VMEM((heads_here, seq_dev, 1), jnp.float32),
@@ -426,9 +458,9 @@
             pltpu.VMEM((n_exp, own, width), bf16),
             pltpu.VMEM((devices, 2 * ROWS, piece), bf16),
             pltpu.VMEM((devices, 2 * ROWS, piece), bf16),
-            pltpu.VMEM((n_ctx, n_exp * ROWS, 2 * hidden_width), bf16),
-            pltpu.VMEM((n_ctx, n_exp * ROWS, 2 * hidden_width), bf16),
-            pltpu.VMEM((n_ctx, n_exp * ROWS, hidden_width), bf16),
+            pltpu.VMEM((n_ctx, 2 * n_exp * CAP, hidden_width), bf16),
+            pltpu.VMEM((n_ctx, 2 * n_exp * CAP, hidden_width), bf16),
+            pltpu.VMEM((n_ctx, 2 * n_exp * CAP, hidden_width // 2), bf16),
             pltpu.VMEM((devices, 2 * ROWS, piece), bf16),
             pltpu.VMEM((devices, 2 * ROWS, piece), bf16),
             dma((4,)),
@@ -449,9 +481,10 @@
             collective_id=0, has_side_effects=True, vmem_limit_bytes=60 * 1024 * 1024
         ),
     )(
-        queries,
-        keys_values,
-        own_tokens,
+        projected,
+        cosines,
+        sines,
+        tokens,
         moe_gain.reshape(1, width),
         send_matrix,
         combine,

time: 77.5 us -> 75 us (0.968)
  Pallas kernels: 64.8 us -> 61.9 us
  local copies, waits for them, and re-layouts: 4.19 us -> 2.58 us
  other arithmetic: 4.2 us -> 5.18 us
  matrix products: 4.05 us -> 4.92 us
    pallas_call x1, Pallas kernels: 64.8 us -> 61.9 us  [body(): pl.pallas_call(functools.partial(layer_kernel, n_ctx, n_exp, pieces), out...]
    dynamic_slice x1 -> x0, local copies, waits for them, and re-layouts: 1.57 us -> none  [body(): lax.dynamic_slice_in_dim(tokens, lax.axis_index('exp') * own, own, 0)]
    dot_general x1, matrix products: 4.05 us -> 4.92 us  [body(): jnp.einsum('sd,dhc->hsc', normed, w_qkv, preferred_element_type=jnp.float32)]
    concatenate x2 -> x1, other arithmetic: 1.57 us -> 0.75 us  [rotary_tables(): jnp.concatenate([cosines, cosines], axis=1)]
    unnamed x7 -> x1, local copies, waits for them, and re-layouts: 1.58 us -> 1.57 us
where the time goes in v3:
time: 75 us; the launch traced here: 74.7 us
  Pallas kernels  61.9 us (83%)
  other arithmetic  5.18 us (7%)
  matrix products  4.92 us (7%)
  local copies, waits for them, and re-layouts  2.58 us (3%)
    pallas_call x1, Pallas kernels, body(): pl.pallas_call(functools.partial(layer_kernel, n_ctx, n_exp, pieces), out...  61.9 us
    dot_general x1, matrix products, body(): jnp.einsum('sd,dhc->hsc', normed, w_qkv, preferred_element_type=jnp.float32)  4.92 us
    unnamed x1, local copies, waits for them, and re-layouts  1.57 us

profile of v3, /device:TPU:0, one launch (start us, length us, event | category | flops | bytes accessed | tf_op | source)
XLA Modules:
  0.0 74.7 jit_solution(1012565601960827050)
XLA Ops:
  0.0 0.7 fusion.13
  0.7 0.7 convert_element_type.19
  1.4 1.2 %fusion.5 = f32[128]{0:T(128)S(1)} fusion(bf16[128,2048]{1,0:T(8,128)(2,1)} %tokens_ref.1), kind=kLoop, calls=%fused_computation.5 | loop fusion | flops 786304 | bytes 524800 | tf_op jit(solution)/shard_map/reduce_sum | solution.py:19
  2.6 0.7 select_reduce_fusion
  3.4 0.1 eq.40
  3.4 0.1 copy.26
  3.5 0.2 convert_reduce_fusion
  3.7 0.1 copy.25
  3.8 0.1 copy.27
  3.9 0.6 broadcast_select_fusion
  4.5 0.7 copy.28.send_matrix_ref
  5.2 0.3 fusion.12
  5.5 0.7 %pad_maximum_fusion = (f32[128,128]{1,0:T(8,128)}, f32[128,128]{1,0:T(8,128)}) fusion(f32[128,64]{1,0:T(8,128)S(1)} %get-tuple-element.9, f32[128,64]{1,0:T(8,128)S(1)} %get-tuple-element.8, f32[128,64]{1,0:T(8,128)S(1)} %get-tuple-element.7), kind=kLoop, calls=%fused_computation.13 | loop fusion | flops 32768 | bytes 229376 | tf_op jit(solution)/shard_map/concatenate | solution.py:27
  6.2 4.9 %fusion.2.projected_ref = f32[4,128,384]{2,1,0:T(8,128)} fusion(bf16[2048,4,384]{2,1,0:T(4,128)(2,1)} %param.14, bf16[128,2048]{1,0:T(8,128)(2,1)} %tokens_ref.1, f32[2048]{0:T(1024)} %param.13, f32[128]{0:T(128)S(1)} %add_rsqrt_fusion), kind=kOutput, calls=%fused_computation.4 | convolution fusion | flops 806354944 | bytes 7610880 | tf_op jit(solution)/shard_map/sd,dhc->hsc/dot_general | solution.py:417
  11.1 61.9 %shard_map.109 = bf16[32,2048]{1,0:T(8,128)(2,1)} custom-call(f32[4,128,384]{2,1,0:T(8,128)} %fusion.2.projected_ref, f32[128,128]{1,0:T(8,128)} %get-tuple-element.10.cosines_ref, f32[128,128]{1,0:T(8,128)} %get-tuple-element.11.sines_ref, bf16[128,2048]{1,0:T(8,128)(2,1)} %tokens_ref.1, f32[1,2048]{1,0:T(1,128)} %bitcast.22, ...), custom_call_target="tpu_custom_call" | custom-call | tf_op jit(solution)/shard_map/pallas_call | solution.py:441
  73.1 1.6 %copy.34 = bf16[32,2048]{1,0:T(8,128)(2,1)} copy(bf16[32,2048]{1,0:T(8,128)(2,1)} %shard_map.109) | data formatting | bytes 262144
  (8 shorter events, 0.0 us)

commit v4 on v3

--- a/solution.py
+++ b/solution.py
@@ -46,18 +46,20 @@
     n_ctx,
     n_exp,
     pieces,
+    groups,
     projected_ref,
     cosines_ref,
     sines_ref,
     tokens_ref,
     gain_ref,
-    send_matrix_ref,
-    combine_ref,
+    ids_ref,
+    probs_ref,
     w_out_hbm,
     w_gate_hbm,
     w_up_hbm,
     w_down_hbm,
     out_ref,
+    combine_ref,
     q_ref,
     kv_buf,
     peak_ref,
@@ -132,11 +134,6 @@
             + pltpu.roll(vectors, head_dim // 2, axis=1) * sines_ref[...]
         ).astype(bf16)
 
-    for head in range(heads):
-        kv_buf[c, head] = rotated(projected_ref[head, :, head_dim : 2 * head_dim])
-        kv_buf[c, heads + head] = projected_ref[head, :, 2 * head_dim :].astype(bf16)
-    pl.semaphore_wait(barrier, devices - 1)
-
     def remote(src, dst, send_sem, recv_sem, device):
         return pltpu.make_async_remote_copy(
             src_ref=src,
@@ -147,18 +144,28 @@
             device_id_type=pl.DeviceIdType.MESH,
         )
 
-    def hop(block):
+    group = heads // groups
+
+    def hop(block, part):
+        heads_of = pl.ds(part * 2 * group, 2 * group)
         return remote(
-            kv_buf.at[block],
-            kv_buf.at[block],
-            kv_send_sem.at[block],
-            kv_recv_sem.at[block],
+            kv_buf.at[block, heads_of],
+            kv_buf.at[block, heads_of],
+            kv_send_sem.at[block, part],
+            kv_recv_sem.at[block, part],
             {"ctx": lax.rem(c + 1, n_ctx)},
         )
 
-    @pl.when(c + 1 < n_ctx)
-    def _():
-        hop(c).start()
+    for part in range(groups):
+        for head in range(part * group, (part + 1) * group):
+            kv_buf[c, 2 * head] = rotated(projected_ref[head, :, head_dim : 2 * head_dim])
+            kv_buf[c, 2 * head + 1] = projected_ref[head, :, 2 * head_dim :].astype(bf16)
+        if part == 0:
+            pl.semaphore_wait(barrier, devices - 1)
+
+        @pl.when(c + 1 < n_ctx)
+        def _():
+            hop(c, part).start()
 
     scale = head_dim ** (-0.5)
     over_last = (((1,), (1,)), ((), ()))
@@ -168,7 +175,7 @@
     for head in range(heads):
         q_ref[head] = rotated(projected_ref[head, :, :head_dim])
         scores = (
-            lax.dot_general(q_ref[head], kv_buf[c, head], over_last, preferred_element_type=f32)
+            lax.dot_general(q_ref[head], kv_buf[c, 2 * head], over_last, preferred_element_type=f32)
             * scale
         )
         scores = jnp.where(allowed, scores, -jnp.inf)
@@ -177,35 +184,61 @@
         peak_ref[head] = peak
         total_ref[head] = jnp.sum(probs, axis=1, keepdims=True)
         sum_ref[head] = jnp.dot(
-            probs.astype(bf16), kv_buf[c, heads + head], preferred_element_type=f32
-        )
+            probs.astype(bf16), kv_buf[c, 2 * head + 1], preferred_element_type=f32
+        )
+
+    slots = n_exp * ROWS
+    slot_of = lax.broadcasted_iota(jnp.int32, (own, slots), 1)
+    marks = jnp.zeros((own, slots), f32)
+    weight = jnp.zeros((own, slots), f32)
+    for k in range(ids_ref.shape[1]):
+        hit = ids_ref[:, k : k + 1] == slot_of // ROWS
+        marks = jnp.where(hit, 1.0, marks)
+        weight = weight + jnp.where(hit, probs_ref[:, k : k + 1], 0.0)
+    before = lax.broadcasted_iota(jnp.int32, (own, own), 1) < lax.broadcasted_iota(
+        jnp.int32, (own, own), 0
+    )
+    place = jnp.dot(
+        before.astype(f32).astype(bf16), marks.astype(bf16), preferred_element_type=f32
+    )
+    in_slot = jnp.where(place == lax.rem(slot_of, ROWS).astype(f32), marks, 0.0)
+    combine_ref[...] = in_slot * weight
+    in_slot = in_slot.astype(bf16)
 
     def earlier_block(step, carry):
         @pl.when(step <= c)
         def _():
             block = c - step
-            hop(block).wait_recv()
-
-            @pl.when(c + 1 < n_ctx)
-            def _():
-                hop(block).start()
-
-            for head in range(heads):
-                scores = (
-                    lax.dot_general(
-                        q_ref[head], kv_buf[block, head], over_last, preferred_element_type=f32
+            for part in range(groups):
+                hop(block, part).wait_recv()
+
+                @pl.when(c + 1 < n_ctx)
+                def _():
+                    hop(block, part).start()
+
+                for head in range(part * group, (part + 1) * group):
+                    scores = (
+                        lax.dot_general(
+                            q_ref[head],
+                            kv_buf[block, 2 * head],
+                            over_last,
+                            preferred_element_type=f32,
+                        )
+                        * scale
                     )
-                    * scale
-                )
-                old_peak = peak_ref[head]
-                peak = jnp.maximum(old_peak, jnp.max(scores, axis=1, keepdims=True))
-                probs = jnp.exp(scores - peak)
-                factor = jnp.exp(old_peak - peak)
-                peak_ref[head] = peak
-                total_ref[head] = total_ref[head] * factor + jnp.sum(probs, axis=1, keepdims=True)
-                sum_ref[head] = sum_ref[head] * factor + jnp.dot(
-                    probs.astype(bf16), kv_buf[block, heads + head], preferred_element_type=f32
-                )
+                    old_peak = peak_ref[head]
+                    peak = jnp.maximum(old_peak, jnp.max(scores, axis=1, keepdims=True))
+                    probs = jnp.exp(scores - peak)
+                    factor = jnp.exp(old_peak - peak)
+                    peak_ref[head] = peak
+                    total_ref[head] = total_ref[head] * factor + jnp.sum(
+                        probs, axis=1, keepdims=True
+                    )
+                    sum_ref[head] = sum_ref[head] * factor + jnp.dot(
+                        probs.astype(bf16),
+                        kv_buf[block, 2 * head + 1],
+                        preferred_element_type=f32,
+                    )
 
         return carry
 
@@ -250,7 +283,9 @@
 
     square = jnp.mean(residual * residual, axis=-1, keepdims=True)
     normed = (residual * lax.rsqrt(square + epsilon) * gain_ref[...]).astype(bf16)
-    outgoing = jnp.dot(send_matrix_ref[...], normed, preferred_element_type=f32)
+    outgoing = lax.dot_general(
+        in_slot, normed, (((0,), (0,)), ((), ())), preferred_element_type=f32
+    )
 
     def packed(rows):
         parts = [
@@ -381,7 +416,8 @@
     def sent_block(step, carry):
         @pl.when(jnp.logical_and(step <= c, c + 1 < n_ctx))
         def _():
-            hop(c - step).wait_send()
+            for part in range(groups):
+                hop(c - step, part).wait_send()
 
         return carry
 
@@ -418,32 +454,22 @@
     cosines, sines = rotary_tables(positions, head_dim)
     own = seq_dev // n_exp
 
-    flight = n_exp
-    hits = expert_ids[:, :, None] == jnp.arange(flight, dtype=jnp.int32)[None, None, :]
-    marks = jnp.any(hits, axis=1)
-    weight = jnp.sum(jnp.where(hits, gate_probs[:, :, None], 0.0), axis=1)
-    before = jnp.arange(own)[:, None] > jnp.arange(own)[None, :]
-    place = jnp.sum((before[:, :, None] & marks[None, :, :]).astype(jnp.int32), axis=1)
-    in_slot = marks[:, :, None] & (
-        place[:, :, None] == jnp.arange(ROWS, dtype=jnp.int32)[None, None, :]
-    )
-    send_matrix = in_slot.reshape(own, flight * ROWS).T.astype(jnp.bfloat16)
-    combine = jnp.where(in_slot, weight[:, :, None], 0.0).reshape(own, flight * ROWS)
-
     columns = width // n_ctx
     pieces = 2 if columns % 256 == 0 else 1
     piece = columns // pieces
+    groups = heads_here
     hidden_width = w_gate.shape[2]
     bf16 = jnp.bfloat16
     vmem = pl.BlockSpec(memory_space=pltpu.VMEM)
     anywhere = pl.BlockSpec(memory_space=pl.ANY)
     dma = pltpu.SemaphoreType.DMA
     return pl.pallas_call(
-        functools.partial(layer_kernel, n_ctx, n_exp, pieces),
+        functools.partial(layer_kernel, n_ctx, n_exp, pieces, groups),
         out_shape=jax.ShapeDtypeStruct((own, width), bf16),
         in_specs=[vmem] * 7 + [anywhere] * 4,
         out_specs=vmem,
         scratch_shapes=[
+            pltpu.VMEM((own, n_exp * ROWS), jnp.float32),
             pltpu.VMEM((heads_here, seq_dev, head_dim), bf16),
             pltpu.VMEM((n_ctx, 2 * heads_here, seq_dev, head_dim), bf16),
             pltpu.VMEM((heads_here, seq_dev, 1), jnp.float32),
@@ -464,8 +490,8 @@
             pltpu.VMEM((devices, 2 * ROWS, piece), bf16),
             pltpu.VMEM((devices, 2 * ROWS, piece), bf16),
             dma((4,)),
-            dma((n_ctx,)),
-            dma((n_ctx,)),
+            dma((n_ctx, groups)),
+            dma((n_ctx, groups)),
             dma((n_exp,)),
             dma((n_exp,)),
             dma((devices,)),
@@ -486,8 +512,8 @@
         sines,
         tokens,
         moe_gain.reshape(1, width),
-        send_matrix,
-        combine,
+        expert_ids,
+        gate_probs,
         w_out.reshape(heads_here * head_dim, width),
         w_gate[0],
         w_up[0],

time: 75 us -> 70.7 us (0.943)
  Pallas kernels: 61.9 us -> 58.2 us
  other arithmetic: 5.18 us -> 2.96 us
  local copies, waits for them, and re-layouts: 2.58 us -> 4.32 us
    pallas_call x1, Pallas kernels: 61.9 us -> 58.2 us  [body(): pl.pallas_call(functools.partial(layer_kernel, n_ctx, n_exp, pieces, grou...]
    unnamed x1 -> x3, local copies, waits for them, and re-layouts: 1.57 us -> 4.32 us
    reduce_sum x2 -> x0, other arithmetic: 0.88 us -> none  [the longest x1 0.73 us: body(): weight = jnp.sum(jnp.where(hits, gate_probs[:, :, None], 0.0), axis=1)]
where the time goes in v4:
time: 70.7 us; the launch traced here: 70.5 us
  Pallas kernels  58.2 us (82%)
  matrix products  4.92 us (7%)
  local copies, waits for them, and re-layouts  4.32 us (6%)
  other arithmetic  2.96 us (4%)
    pallas_call x1, Pallas kernels, body(): pl.pallas_call(functools.partial(layer_kernel, n_ctx, n_exp, pieces, grou...  58.2 us
    dot_general x1, matrix products, body(): jnp.einsum('sd,dhc->hsc', normed, w_qkv, preferred_element_type=jnp.float32)  4.92 us
    unnamed x3, local copies, waits for them, and re-layouts  4.32 us

profile of v4, /device:TPU:0, one launch (start us, length us, event | category | flops | bytes accessed | tf_op | source)
XLA Modules:
  0.0 70.5 jit_solution(5622131092032795981)
XLA Ops:
  0.0 0.7 convert_element_type.11
  0.7 1.2 %fusion.5 = f32[128]{0:T(128)S(1)} fusion(bf16[128,2048]{1,0:T(8,128)(2,1)} %tokens_ref.1), kind=kLoop, calls=%fused_computation.5 | loop fusion | flops 786304 | bytes 524800 | tf_op jit(solution)/shard_map/reduce_sum | solution.py:19
  1.9 1.4 %copy.13.ids_ref = s32[32,6]{1,0:T(8,128)} copy(s32[32,6]{0,1:T(8,128)} %param.17) | data formatting | bytes 1536 | tf_op args[6]
  3.3 1.4 %copy.14.probs_ref = f32[32,6]{1,0:T(8,128)} copy(f32[32,6]{0,1:T(8,128)} %param.18) | data formatting | bytes 1536 | tf_op args[7]
  4.7 0.3 fusion.12
  5.0 0.7 %pad_maximum_fusion = (f32[128,128]{1,0:T(8,128)}, f32[128,128]{1,0:T(8,128)}) fusion(f32[128,64]{1,0:T(8,128)S(1)} %get-tuple-element.7, f32[128,64]{1,0:T(8,128)S(1)} %get-tuple-element.6, f32[128,64]{1,0:T(8,128)S(1)} %get-tuple-element.5), kind=kLoop, calls=%fused_computation.13 | loop fusion | flops 32768 | bytes 229376 | tf_op jit(solution)/shard_map/concatenate | solution.py:27
  5.7 4.9 %fusion.2.projected_ref = f32[4,128,384]{2,1,0:T(8,128)} fusion(bf16[2048,4,384]{2,1,0:T(4,128)(2,1)} %param.14, bf16[128,2048]{1,0:T(8,128)(2,1)} %tokens_ref.1, f32[2048]{0:T(1024)} %param.13, f32[128]{0:T(128)S(1)} %add_rsqrt_fusion), kind=kOutput, calls=%fused_computation.4 | convolution fusion | flops 806354944 | bytes 7610880 | tf_op jit(solution)/shard_map/sd,dhc->hsc/dot_general | solution.py:453
  10.6 58.2 %shard_map.109 = bf16[32,2048]{1,0:T(8,128)(2,1)} custom-call(f32[4,128,384]{2,1,0:T(8,128)} %fusion.2.projected_ref, f32[128,128]{1,0:T(8,128)} %get-tuple-element.8.cosines_ref, f32[128,128]{1,0:T(8,128)} %get-tuple-element.9.sines_ref, bf16[128,2048]{1,0:T(8,128)(2,1)} %tokens_ref.1, f32[1,2048]{1,0:T(1,128)} %bitcast.14, s32[32,6]{1,0:T(8,128)} %copy.13.ids_ref, ...), custom_call_target="tpu_custom_call" | custom-call | tf_op jit(solution)/shard_map/pallas_call | solution.py:466
  68.9 1.6 %copy.20 = bf16[32,2048]{1,0:T(8,128)(2,1)} copy(bf16[32,2048]{1,0:T(8,128)(2,1)} %shard_map.109) | data formatting | bytes 262144
  (2 shorter events, 0.0 us)

commit v5 on v4

--- a/solution.py
+++ b/solution.py
@@ -20,13 +20,11 @@
 
 
 def rotary_tables(positions, width):
-    freqs = 10000.0 ** (-jnp.arange(width // 2, dtype=jnp.float32) * 2.0 / width)
+    half = width // 2
+    column = jnp.arange(width, dtype=jnp.int32)
+    freqs = 10000.0 ** (-(column % half).astype(jnp.float32) * 2.0 / width)
     angles = positions.astype(jnp.float32)[:, None] * freqs[None, :]
-    cosines, sines = jnp.cos(angles), jnp.sin(angles)
-    return (
-        jnp.concatenate([cosines, cosines], axis=1),
-        jnp.concatenate([-sines, sines], axis=1),
-    )
+    return (jnp.cos(angles), jnp.where(column < half, -1.0, 1.0)[None, :] * jnp.sin(angles))
 
 
 def each(begin, end, step):
@@ -188,21 +186,21 @@
         )
 
     slots = n_exp * ROWS
-    slot_of = lax.broadcasted_iota(jnp.int32, (own, slots), 1)
-    marks = jnp.zeros((own, slots), f32)
-    weight = jnp.zeros((own, slots), f32)
-    for k in range(ids_ref.shape[1]):
-        hit = ids_ref[:, k : k + 1] == slot_of // ROWS
+    slot_of = lax.broadcasted_iota(jnp.int32, (slots, own), 0)
+    marks = jnp.zeros((slots, own), f32)
+    weight = jnp.zeros((slots, own), f32)
+    for k in range(ids_ref.shape[0]):
+        hit = ids_ref[k : k + 1, :] == slot_of // ROWS
         marks = jnp.where(hit, 1.0, marks)
-        weight = weight + jnp.where(hit, probs_ref[:, k : k + 1], 0.0)
-    before = lax.broadcasted_iota(jnp.int32, (own, own), 1) < lax.broadcasted_iota(
-        jnp.int32, (own, own), 0
+        weight = weight + jnp.where(hit, probs_ref[k : k + 1, :], 0.0)
+    before = lax.broadcasted_iota(jnp.int32, (own, own), 0) < lax.broadcasted_iota(
+        jnp.int32, (own, own), 1
     )
     place = jnp.dot(
-        before.astype(f32).astype(bf16), marks.astype(bf16), preferred_element_type=f32
+        marks.astype(bf16), before.astype(f32).astype(bf16), preferred_element_type=f32
     )
     in_slot = jnp.where(place == lax.rem(slot_of, ROWS).astype(f32), marks, 0.0)
-    combine_ref[...] = in_slot * weight
+    combine_ref[...] = (in_slot * weight).T
     in_slot = in_slot.astype(bf16)
 
     def earlier_block(step, carry):
@@ -283,9 +281,7 @@
 
     square = jnp.mean(residual * residual, axis=-1, keepdims=True)
     normed = (residual * lax.rsqrt(square + epsilon) * gain_ref[...]).astype(bf16)
-    outgoing = lax.dot_general(
-        in_slot, normed, (((0,), (0,)), ((), ())), preferred_element_type=f32
-    )
+    outgoing = jnp.dot(in_slot, normed, preferred_element_type=f32)
 
     def packed(rows):
         parts = [
@@ -512,8 +508,8 @@
         sines,
         tokens,
         moe_gain.reshape(1, width),
-        expert_ids,
-        gate_probs,
+        expert_ids.T,
+        gate_probs.T,
         w_out.reshape(heads_here * head_dim, width),
         w_gate[0],
         w_up[0],

time: 70.7 us -> 67.8 us (0.959)
  local copies, waits for them, and re-layouts: 4.32 us -> 1.57 us
    unnamed x3 -> x1, local copies, waits for them, and re-layouts: 4.32 us -> 1.57 us
    mul x0 -> x1, other arithmetic: none -> 0.98 us  [rotary_tables(): jnp.where(column < half, -1.0, 1.0)[None, :] * jnp.sin(angles)]
    concatenate x1 -> x0, other arithmetic: 0.75 us -> none  [rotary_tables(): jnp.concatenate([cosines, cosines], axis=1)]
where the time goes in v5:
time: 67.8 us; the launch traced here: 67.6 us
  Pallas kernels  58.2 us (86%)
  matrix products  4.92 us (7%)
  other arithmetic  2.88 us (4%)
  local copies, waits for them, and re-layouts  1.57 us (2%)
    pallas_call x1, Pallas kernels, body(): pl.pallas_call(functools.partial(layer_kernel, n_ctx, n_exp, pieces, grou...  58.2 us
    dot_general x1, matrix products, body(): jnp.einsum('sd,dhc->hsc', normed, w_qkv, preferred_element_type=jnp.float32)  4.92 us
    unnamed x1, local copies, waits for them, and re-layouts  1.57 us

profile of v5, /device:TPU:0, one launch (start us, length us, event | category | flops | bytes accessed | tf_op | source)
XLA Modules:
  0.0 67.6 jit_solution(351732497992913560)
XLA Ops:
  0.0 0.7 convert_element_type.18
  0.7 1.2 %fusion.5 = f32[128]{0:T(128)S(1)} fusion(bf16[128,2048]{1,0:T(8,128)(2,1)} %tokens_ref.1), kind=kLoop, calls=%fused_computation.5 | loop fusion | flops 786304 | bytes 524800 | tf_op jit(solution)/shard_map/reduce_sum | solution.py:19
  1.9 1.0 %fusion.12 = (f32[128,128]{1,0:T(8,128)}, f32[128,128]{1,0:T(8,128)}) fusion(f32[128]{0:T(128)S(1)} %get-tuple-element.7, f32[128]{0:T(128)S(1)} %get-tuple-element.8, f32[128]{0:T(128)S(1)} %convert_element_type.18), kind=kLoop, calls=%fused_computation.13 | loop fusion | flops 32768 | bytes 132608 | tf_op jit(solution)/shard_map/mul | solution.py:27
  2.9 4.9 %fusion.2.projected_ref = f32[4,128,384]{2,1,0:T(8,128)} fusion(bf16[2048,4,384]{2,1,0:T(4,128)(2,1)} %param.14, bf16[128,2048]{1,0:T(8,128)(2,1)} %tokens_ref.1, f32[2048]{0:T(1024)} %param.13, f32[128]{0:T(128)S(1)} %add_rsqrt_fusion), kind=kOutput, calls=%fused_computation.4 | convolution fusion | flops 806354944 | bytes 7610880 | tf_op jit(solution)/shard_map/sd,dhc->hsc/dot_general | solution.py:449
  7.8 58.2 %shard_map.109 = bf16[32,2048]{1,0:T(8,128)(2,1)} custom-call(f32[4,128,384]{2,1,0:T(8,128)} %fusion.2.projected_ref, f32[128,128]{1,0:T(8,128)} %get-tuple-element.6.cosines_ref, f32[128,128]{1,0:T(8,128)} %get-tuple-element.5.sines_ref, bf16[128,2048]{1,0:T(8,128)(2,1)} %tokens_ref.1, f32[1,2048]{1,0:T(1,128)} %bitcast.16, s32[6,32]{1,0:T(8,128)} %bitcast.17, ...), custom_call_target="tpu_custom_call" | custom-call | tf_op jit(solution)/shard_map/pallas_call | solution.py:462
  66.0 1.6 %copy.18 = bf16[32,2048]{1,0:T(8,128)(2,1)} copy(bf16[32,2048]{1,0:T(8,128)(2,1)} %shard_map.109) | data formatting | bytes 262144
  (2 shorter events, 0.0 us)
